TPU v7x, 32 devices: a whole 2x2x4 slice. The times are simulated.
32 devices in a mesh: dp: 16 (over z, y, core), tensor: 2 (over x).
Axes of the slice: x: 2, y: 2, z: 4, core: 2. Of those that a mesh axis runs over, the one named last changes fastest.
Arguments:
- tokens: bfloat16 [32, 256, 768], P('dp'), may hold values from -6 to 6
- segment_ids: int32 [32, 256], P('dp'), may hold values from 0 to 5, never falling along the last dimension, each value on 1 to 64 neighbouring positions
- w_qkv: bfloat16 [768, 3, 768], P(None, None, 'tensor'), may hold values from -0.21875 to 0.21875
- qv_bias: bfloat16 [2, 768], P(None, 'tensor'), may hold values from -3 to 3
- w_out: bfloat16 [768, 768], P(None, 'tensor'), may hold values from -0.625 to 0.625
- out_bias: bfloat16 [768], replicated, may hold values from -2 to 2
- w_in: bfloat16 [768, 3072], P(None, 'tensor'), may hold values from -0.21875 to 0.21875
- hidden_bias: bfloat16 [3072], P('tensor'), may hold values from -3 to 3
- w_down: bfloat16 [768, 3072], P(None, 'tensor'), may hold values from -0.15625 to 0.15625
- mlp_bias: bfloat16 [768], replicated, may hold values from -2 to 2
- ln_gain: bfloat16 [2, 768], replicated, may hold values from 0.5 to 1.5
- ln_bias: bfloat16 [2, 768], replicated, may hold values from -2 to 2
- cotangent: bfloat16 [32, 256, 768], P('dp'), may hold values from -6 to 6
Outputs:
- block_out: bfloat16 [32, 256, 768], P('dp')
- grad_tokens: bfloat16 [32, 256, 768], P('dp')
- grad_w_qkv: float32 [768, 3, 768], P('dp', None, 'tensor')
- grad_qv_bias: float32 [2, 768], P(None, 'tensor')
- grad_w_out: float32 [768, 768], P('dp', 'tensor')
- grad_out_bias: float32 [768], replicated
- grad_w_in: float32 [768, 3072], P('dp', 'tensor')
- grad_hidden_bias: float32 [3072], P('tensor')
- grad_w_down: float32 [768, 3072], P('dp', 'tensor')
- grad_mlp_bias: float32 [768], replicated
- grad_ln_gain: float32 [2, 768], replicated
- grad_ln_bias: float32 [2, 768], replicated
Inputs may be any that keep to these rules, and one draw needn't show every extreme that they name: `segment_ids`: along each packed sequence the ids never fall; each image holds 1 to 64 consecutive tokens, and in each sequence some image holds exactly 64.
All inputs are finite; a program needn't handle non-finite values.
Results may differ from a plain program's by a relative error of at most 0.017.
Values may be sent and summed in bfloat16 or wider, within the bound.
A program may use at most 128 MiB of HBM per device.

v0:
```python
import jax
import jax.numpy as jnp
from jax import lax
from jax.sharding import PartitionSpec as P

HEAD_DIM = 64


norm_eps = 1e-06
masked_score = -1000000000.0


def layer_norm(values, gain, shift):
    center = values - jnp.mean(values, axis=-1, keepdims=True)
    spread = jnp.mean(center * center, axis=-1, keepdims=True)
    return center * lax.rsqrt(spread + norm_eps) * gain + shift


def gelu_exact(values):
    return jax.nn.gelu(values, approximate=False)


def body(
    tokens,
    segment_ids,
    w_qkv,
    qv_bias,
    w_out,
    out_bias,
    w_in,
    hidden_bias,
    w_down,
    mlp_bias,
    ln_gain,
    ln_bias,
    cotangent,
):
    seq_count, seq_len, model_width = tokens.shape
    row_count = seq_count * seq_len
    local_width = w_qkv.shape[2]
    local_heads = local_width // HEAD_DIM
    score_scale = HEAD_DIM ** (-0.5)
    head_shape = (seq_count, seq_len, local_heads, HEAD_DIM)
    contract_last = (((1,), (1,)), ((), ()))
    contract_first = (((0,), (0,)), ((), ()))
    gains = ln_gain.astype(jnp.float32)
    shifts = ln_bias.astype(jnp.float32)
    bias_pair = qv_bias.astype(jnp.float32)
    inputs = tokens.reshape(row_count, model_width).astype(jnp.float32)
    normed_one, norm_one_back = jax.vjp(layer_norm, inputs, gains[0], shifts[0])
    normed_one_low = normed_one.astype(jnp.bfloat16)
    projected = jnp.einsum("rd,dce->rce", normed_one_low, w_qkv, preferred_element_type=jnp.float32)
    query = (projected[:, 0] + bias_pair[0]).astype(jnp.bfloat16).reshape(head_shape)
    keys_low = projected[:, 1].astype(jnp.bfloat16).reshape(head_shape)
    values_low = (projected[:, 2] + bias_pair[1]).astype(jnp.bfloat16).reshape(head_shape)
    allowed = segment_ids[:, None, :, None] == segment_ids[:, None, None, :]

    def masked_scores():
        raw_scores = (
            jnp.einsum("sqhe,skhe->shqk", query, keys_low, preferred_element_type=jnp.float32)
            * score_scale
        )
        return jnp.where(allowed, raw_scores, masked_score)

    scores = masked_scores()
    top_score = jnp.max(scores, axis=-1, keepdims=True)
    expo = jnp.exp(scores - top_score)
    total = jnp.sum(expo, axis=-1, keepdims=True)
    log_total = top_score + jnp.log(total)
    soft_low = (expo / total).astype(jnp.bfloat16)
    heads_out = jnp.einsum(
        "shqk,skhe->sqhe", soft_low, values_low, preferred_element_type=jnp.float32
    )
    heads_out = heads_out.reshape(row_count, local_width).astype(jnp.bfloat16)
    attn_partial = lax.dot_general(
        heads_out, w_out, contract_last, preferred_element_type=jnp.float32
    )
    attended = lax.psum(attn_partial.astype(jnp.bfloat16), "tensor").astype(
        jnp.float32
    ) + out_bias.astype(jnp.float32)
    resid = inputs + attended
    normed_two, norm_two_back = jax.vjp(layer_norm, resid, gains[1], shifts[1])
    normed_two_low = normed_two.astype(jnp.bfloat16)
    hidden_pre = jnp.dot(
        normed_two_low, w_in, preferred_element_type=jnp.float32
    ) + hidden_bias.astype(jnp.float32)
    active, gelu_back = jax.vjp(gelu_exact, hidden_pre)
    active_low = active.astype(jnp.bfloat16)
    mlp_partial = lax.dot_general(
        active_low, w_down, contract_last, preferred_element_type=jnp.float32
    )
    mlp_result = lax.psum(mlp_partial.astype(jnp.bfloat16), "tensor").astype(
        jnp.float32
    ) + mlp_bias.astype(jnp.float32)
    block_out = (resid + mlp_result).astype(jnp.bfloat16).reshape(seq_count, seq_len, model_width)
    grad_low = cotangent.reshape(row_count, model_width)
    grad_float = grad_low.astype(jnp.float32)
    grad_mlp_bias = jnp.sum(grad_float, axis=0)
    grad_down = lax.dot_general(
        grad_low, active_low, contract_first, preferred_element_type=jnp.float32
    )
    grad_active = jnp.dot(grad_low, w_down, preferred_element_type=jnp.float32)
    (grad_pre,) = gelu_back(grad_active)
    grad_pre_low = grad_pre.astype(jnp.bfloat16)
    grad_hidden_bias = jnp.sum(grad_pre_low.astype(jnp.float32), axis=0)
    grad_in = lax.dot_general(
        normed_two_low, grad_pre_low, contract_first, preferred_element_type=jnp.float32
    )
    grad_normed_two = lax.psum(
        lax.dot_general(
            grad_pre_low, w_in, contract_last, preferred_element_type=jnp.float32
        ).astype(jnp.bfloat16),
        "tensor",
    ).astype(jnp.float32)
    grad_resid_two, grad_gain_two, grad_shift_two = norm_two_back(grad_normed_two)
    grad_resid = grad_float + grad_resid_two
    grad_out_bias = jnp.sum(grad_resid, axis=0)
    grad_resid_low = grad_resid.astype(jnp.bfloat16)
    grad_wout = lax.dot_general(
        grad_resid_low, heads_out, contract_first, preferred_element_type=jnp.float32
    )
    grad_heads = (
        jnp.dot(grad_resid_low, w_out, preferred_element_type=jnp.float32)
        .astype(jnp.bfloat16)
        .reshape(head_shape)
    )
    soft_again = jnp.exp(masked_scores() - log_total)
    soft_again_low = soft_again.astype(jnp.bfloat16)
    grad_values = jnp.einsum(
        "shqk,sqhe->skhe", soft_again_low, grad_heads, preferred_element_type=jnp.float32
    )
    grad_soft = jnp.einsum(
        "sqhe,skhe->shqk", grad_heads, values_low, preferred_element_type=jnp.float32
    )
    row_delta = jnp.sum(soft_again * grad_soft, axis=-1, keepdims=True)
    grad_scores = (soft_again * (grad_soft - row_delta)).astype(jnp.bfloat16)
    grad_query = (
        jnp.einsum("shqk,skhe->sqhe", grad_scores, keys_low, preferred_element_type=jnp.float32)
        * score_scale
    )
    grad_keys = (
        jnp.einsum("shqk,sqhe->skhe", grad_scores, query, preferred_element_type=jnp.float32)
        * score_scale
    )
    grad_query_low = grad_query.reshape(row_count, local_width).astype(jnp.bfloat16)
    grad_keys_low = grad_keys.reshape(row_count, local_width).astype(jnp.bfloat16)
    grad_values_low = grad_values.reshape(row_count, local_width).astype(jnp.bfloat16)
    grad_mixed = jnp.stack([grad_query_low, grad_keys_low, grad_values_low], axis=1)
    grad_bias_pair = jnp.stack(
        [
            jnp.sum(grad_query_low.astype(jnp.float32), axis=0),
            jnp.sum(grad_values_low.astype(jnp.float32), axis=0),
        ]
    )
    grad_wqkv = jnp.einsum(
        "rd,rce->dce", normed_one_low, grad_mixed, preferred_element_type=jnp.float32
    )
    grad_normed_one = lax.psum(
        jnp.einsum("rce,dce->rd", grad_mixed, w_qkv, preferred_element_type=jnp.float32).astype(
            jnp.bfloat16
        ),
        "tensor",
    ).astype(jnp.float32)
    grad_inputs_one, grad_gain_one, grad_shift_one = norm_one_back(grad_normed_one)
    grad_tokens = (
        (grad_resid + grad_inputs_one).astype(jnp.bfloat16).reshape(seq_count, seq_len, model_width)
    )
    summed_qkv, summed_out, summed_in, summed_down = (
        lax.psum_scatter(grad_wqkv, "dp", scatter_dimension=0, tiled=True),
        lax.psum_scatter(grad_wout, "dp", scatter_dimension=0, tiled=True),
        lax.psum_scatter(grad_in, "dp", scatter_dimension=0, tiled=True),
        lax.psum_scatter(grad_down, "dp", scatter_dimension=0, tiled=True),
    )
    small_sums = lax.psum(
        (
            grad_bias_pair,
            grad_out_bias,
            grad_hidden_bias,
            grad_mlp_bias,
            jnp.stack([grad_gain_one, grad_gain_two]),
            jnp.stack([grad_shift_one, grad_shift_two]),
        ),
        "dp",
    )
    return (
        block_out,
        grad_tokens,
        summed_qkv,
        small_sums[0],
        summed_out,
        small_sums[1],
        summed_in,
        small_sums[2],
        summed_down,
        small_sums[3],
        small_sums[4],
        small_sums[5],
    )


def solution(mesh):
    return jax.shard_map(
        body,
        mesh=mesh,
        in_specs=(
            P("dp", None, None),
            P("dp", None),
            P(None, None, "tensor"),
            P(None, "tensor"),
            P(None, "tensor"),
            P(),
            P(None, "tensor"),
            P("tensor"),
            P(None, "tensor"),
            P(),
            P(),
            P(),
            P("dp", None, None),
        ),
        out_specs=(
            P("dp", None, None),
            P("dp", None, None),
            P("dp", None, "tensor"),
            P(None, "tensor"),
            P("dp", "tensor"),
            P(),
            P("dp", "tensor"),
            P("tensor"),
            P("dp", "tensor"),
            P(),
            P(),
            P(),
        ),
        check_vma=False,
    )
```

profile of v0, /device:TPU:0, one launch (start us, length us, event | category | flops | bytes accessed | tf_op | source)
XLA Modules:
  0.0 507.6 jit_solution(14296081238358856506)
XLA Ops:
  21.0 2.4 copy.89
  32.9 36.5 %all-reduce.6.cloned.1.call-done = bf16[512,768]{1,0:T(8,128)(2,1)} async-done(((bf16[512,768]{1,0:T(8,128)(2,1)}), bf16[512,768]{1,0:T(8,128)(2,1)}) %all-reduce.6.cloned.1.call-update) | async-done | bytes 786448 | tf_op jit(solution)/shard_map/psum | solution.py:78
  74.3 10.1 %convert_reduce_fusion = (f32[1536]{0:T(1024)}, bf16[512,1536]{1,0:T(8,128)(2,1)S(1)}, f32[512,1536]{1,0:T(8,128)}) fusion(f32[512,1536]{1,0:T(8,128)S(1)} %convolution_add_fusion, bf16[512,768]{1,0:T(8,128)(2,1)S(1)} %bitcast.96, bf16[768,1536]{1,0:T(8,128)(2,1)S(1)} %copy-done), kind=kOutput, calls=%fused_computation.4 | convolution fusion | flops 1266153984 | bytes 11016192 | tf_op jit(solution)/shard_map/dot_general | solution.py:102
  85.5 2.3 convolution_convert_fusion
  88.1 3.6 multiply_convert_fusion.1
  92.8 2.3 convolution_convert_fusion.1
  95.1 27.2 %all-reduce.8.cloned.1.call-done = bf16[512,768]{1,0:T(8,128)(2,1)} async-done(((bf16[512,768]{1,0:T(8,128)(2,1)}), bf16[512,768]{1,0:T(8,128)(2,1)}) %all-reduce.8.cloned.1.call-update) | async-done | bytes 786448 | tf_op jit(solution)/shard_map/psum | solution.py:109
  122.4 2.8 convert_reduce_fusion.2
  131.5 3.3 convert_reduce_fusion.5
  140.5 2.0 convert_element_type.218
  150.2 1.9 copy.106
  152.1 4.0 bitcast_convert_fusion
  156.2 3.1 fusion.44
  159.5 4.4 fusion.38
  164.6 5.5 %fusion.61 = f32[768,1536]{1,0:T(8,128)} fusion(bf16[512,1536]{1,0:T(8,128)(2,1)} %copy-done.22, f32[512,768]{1,0:T(8,128)} %copy-done.4, f32[768]{0:T(1024)S(1)} %get-tuple-element.70, f32[768]{0:T(1024)S(1)} %get-tuple-element.104, f32[512]{0:T(512)S(1)} %copy-done.28), kind=kOutput, calls=%fused_computation.124 | convolution fusion | flops 1209532416 | bytes 7872512 | tf_op jit(solution)/shard_map/dot_general | solution.py:106
  170.2 5.3 %convolution_bitcast_fusion = f32[768,1536]{0,1:T(8,128)} fusion(bf16[512,1536]{1,0:T(8,128)(2,1)} %copy-done.7, bf16[512,768]{1,0:T(8,128)(2,1)} %bitcast.95), kind=kOutput, calls=%fused_computation.1 | convolution fusion | flops 1207959552 | bytes 7077888 | tf_op jit(solution)/shard_map/dot_general | solution.py:99
  175.5 6.1 %copy.116 = f32[768,1536]{1,0:T(8,128)} copy(f32[768,1536]{0,1:T(8,128)} %convolution_bitcast_fusion) | data formatting | bytes 9437184
  183.9 24.1 %all-reduce.10.cloned.1.call-done = (bf16[512,768]{1,0:T(8,128)(2,1)}, bf16[512,768]{1,0:T(8,128)(2,1)}) async-done(((bf16[512,768]{1,0:T(8,128)(2,1)}, bf16[512,768]{1,0:T(8,128)(2,1)}), (bf16[512,768]{1,0:T(8,128)(2,1)}, bf16[512,768]{1,0:T(8,128)(2,1)})) %all-reduce.10.cloned.1.call-update) | async-done | bytes 1572880 | tf_op jit(solution)/shard_map/psum | solution.py:92
  209.7 2.1 fusion.15
  211.8 61.9 %all-reduce = (f32[2,384]{1,0:T(2,128)}, f32[768]{0:T(1024)}, f32[1536]{0:T(1024)}, f32[768]{0:T(1024)}, f32[2,768]{1,0:T(2,128)}, /*index=5*/f32[2,768]{1,0:T(2,128)}) all-reduce(f32[2,384]{1,0:T(2,128)S(1)} %pad_maximum_fusion.5, f32[768]{0:T(1024)S(1)} %copy-done.43, ...), channel_id=1, replica_groups=mesh['dp'=16,'tensor'=2] {'dp'}, use_global_device_ids=true, to_apply=%region_18.19 | all-reduce | flops 6912 | bytes 55296 | tf_op jit(solution)/shard_map/psum | solution.py:174
  273.7 4.1 add_convert_fusion.1
  277.8 64.7 %reduce-scatter.7.cloned.1.call-done = f32[48,3,384]{2,0,1:T(8,128)} async-done(((f32[768,3,384]{2,0,1:T(8,128)}), f32[48,3,384]{2,0,1:T(8,128)}) %reduce-scatter.7.cloned.1.call-update) | async-done | bytes 221200 | tf_op jit(solution)/shard_map/reduce_scatter | solution.py:169
  342.5 79.2 %reduce-scatter.11.cloned.1.call-done = f32[48,1536]{1,0:T(8,128)} async-done(((f32[768,1536]{1,0:T(8,128)}), f32[48,1536]{1,0:T(8,128)}) %reduce-scatter.11.cloned.1.call-update) | async-done | bytes 294928 | tf_op jit(solution)/shard_map/reduce_scatter | solution.py:171
  421.7 79.0 %reduce-scatter.13.cloned.1.call-done = f32[48,1536]{1,0:T(8,128)} async-done(((f32[768,1536]{1,0:T(8,128)}), f32[48,1536]{1,0:T(8,128)}) %reduce-scatter.13.cloned.1.call-update) | async-done | bytes 294928
  (189 shorter events, 54.9 us)
Async XLA Ops:
  7.2 67.0 %copy-start = (bf16[768,1536]{1,0:T(8,128)(2,1)S(1)}, bf16[768,1536]{1,0:T(8,128)(2,1)}, u32[]{:S(2)}) copy-start(bf16[768,1536]{1,0:T(8,128)(2,1)} %param.21) | copy-start | bytes 7077892
  7.2 62.2 %all-reduce.6.cloned.1.call-start = ((), (), s32[]{:S(2)}) async-start(), calls=%async_computation.4 | async-start | bytes 1572864 | tf_op jit(solution)/shard_map/psum | solution.py:78
  7.2 6.6 %copy-start.51 = (bf16[768,3,384]{2,0,1:T(8,128)(2,1)S(1)}, bf16[768,3,384]{2,0,1:T(8,128)(2,1)}, u32[]{:S(2)}) copy-start(bf16[768,3,384]{2,0,1:T(8,128)(2,1)} %param.15) | copy-start | bytes 5308420
  8.7 3.6 copy-start.29
  17.1 7.9 %copy-start.31 = (f32[6,64]{1,0:T(8,128)}, f32[6,64]{1,0:T(8,128)S(1)}, u32[]{:S(2)}) copy-start(f32[6,64]{1,0:T(8,128)S(1)} %add.145) | copy-start | bytes 4612
  21.0 5.9 %copy-start.15 = (bf16[2,256,6,64]{1,0,3,2:T(2,128)(2,1)}, bf16[2,256,6,64]{1,0,3,2:T(2,128)(2,1)S(1)}, u32[]{:S(2)}) copy-start(bf16[2,256,6,64]{1,0,3,2:T(2,128)(2,1)S(1)} %convert_element_type.187) | copy-start | bytes 1179652
  29.4 40.0 %copy-start.3 = (bf16[2,256,768]{2,1,0:T(8,128)(2,1)S(1)}, bf16[2,256,768]{2,1,0:T(8,128)(2,1)}, u32[]{:S(2)}) copy-start(bf16[2,256,768]{2,1,0:T(8,128)(2,1)} %param.13) | copy-start | bytes 2359300
  32.2 90.1 %all-reduce.8.cloned.1.call-start = ((), (), s32[]{:S(2)}) async-start(), calls=%async_computation.5 | async-start | bytes 1572864 | tf_op jit(solution)/shard_map/psum | solution.py:109
  72.6 53.9 %copy-start.27 = (f32[512]{0:T(512)}, f32[512]{0:T(512)S(1)}, u32[]{:S(2)}) copy-start(f32[512]{0:T(512)S(1)} %fusion.56) | copy-start | bytes 6148
  74.1 10.3 %copy-start.19 = (f32[512,1536]{1,0:T(8,128)}, f32[512,1536]{1,0:T(8,128)S(1)}, u32[]{:S(2)}) copy-start(f32[512,1536]{1,0:T(8,128)S(1)} %convolution_add_fusion) | copy-start | bytes 9437188
  87.9 120.1 %all-reduce.10.cloned.1.call-start = ((), (), s32[]{:S(2)}) async-start(), calls=%async_computation.10 | async-start | bytes 3145728 | tf_op jit(solution)/shard_map/psum | solution.py:92
  122.4 4.2 copy-start.12
  131.5 3.4 copy-start.2
  131.5 3.4 copy-start.18
  152.1 4.1 copy-start.14
  156.1 121.6 %reduce-scatter.9.cloned.1.call-start = ((), (), s32[]{:S(2)}) async-start(), calls=%async_computation.7 | async-start | bytes 1253376 | tf_op jit(solution)/shard_map/reduce_scatter | solution.py:170
  159.3 183.2 %reduce-scatter.7.cloned.1.call-start = ((), (), s32[]{:S(2)}) async-start(), calls=%async_computation.6 | async-start | bytes 3760128 | tf_op jit(solution)/shard_map/reduce_scatter | solution.py:169
  164.0 257.7 %reduce-scatter.11.cloned.1.call-start = ((), (), s32[]{:S(2)}) async-start(), calls=%async_computation.8 | async-start | bytes 5013504 | tf_op jit(solution)/shard_map/reduce_scatter | solution.py:171
  170.2 330.5 %reduce-scatter.13.cloned.1.call-start = ((), (), s32[]{:S(2)}) async-start(), calls=%async_computation.9 | async-start | bytes 5013504
  181.7 26.3 %copy-start.30 = (f32[1,2,2,128]{3,1,2,0:T(2,128)S(1)}, f32[1,2,2,128]{3,1,2,0:T(2,128)}, u32[]{:S(2)}) copy-start(f32[1,2,2,128]{3,1,2,0:T(2,128)} %copy-done.29) | copy-start | bytes 6148
  182.3 27.3 %copy-start.36 = (f32[1,2,2,128]{3,1,2,0:T(2,128)S(1)}, f32[1,2,2,128]{3,1,2,0:T(2,128)}, u32[]{:S(2)}) copy-start(f32[1,2,2,128]{3,1,2,0:T(2,128)} %copy-done.35) | copy-start | bytes 6148
  182.3 27.3 %copy-start.34 = (f32[512]{0:T(512)S(1)}, f32[512]{0:T(512)}, u32[]{:S(2)}) copy-start(f32[512]{0:T(512)} %copy-done.33) | copy-start | bytes 6148
  182.3 29.5 %copy-start.43 = (f32[768]{0:T(1024)S(1)}, f32[768]{0:T(1024)}, u32[]{:S(2)}) copy-start(f32[768]{0:T(1024)} %get-tuple-element.85) | copy-start | bytes 9220
  182.3 29.5 %copy-start.45 = (f32[1536]{0:T(1024)S(1)}, f32[1536]{0:T(1024)}, u32[]{:S(2)}) copy-start(f32[1536]{0:T(1024)} %get-tuple-element.82) | copy-start | bytes 18436
  (35 other events, 66.0 us)
Sparse Core Ops, SparseCore 0:
  32.3 37.0 all-reduce.5
  88.0 34.3 all-reduce.7
  156.2 51.6 all-reduce.9
  212.4 58.1 reduce-scatter.8
  275.5 66.9 reduce-scatter.6
  347.2 74.3 reduce-scatter.10
  426.1 74.5 reduce-scatter.12
where the time goes:
time: 509 us; the launch traced here: 508 us
  waiting for transfers between devices  311 us (61%)
  blocking collectives  61.9 us (12%)
  matrix products  50.9 us (10%)
  local copies, waits for them, and re-layouts  38.8 us (8%)
  other arithmetic  29.7 us (6%)
  between operations  14.8 us (3%)
    reduce_scatter x1, waiting for transfers between devices, body(): lax.psum_scatter(grad_in, 'dp', scatter_dimension=0, tiled=True)  79.2 us
    unnamed x8, waiting for transfers between devices  79.2 us
    reduce_scatter x1, waiting for transfers between devices, body(): lax.psum_scatter(grad_wqkv, 'dp', scatter_dimension=0, tiled=True)  64.7 us
    psum x1, blocking collectives, body(): lax.psum((grad_bias_pair, grad_out_bias, grad_hidden_bias, grad_mlp_bias,...  61.9 us
    psum x1, waiting for transfers between devices, body(): lax.psum(attn_partial.astype(jnp.bfloat16), 'tensor').astype(jnp.float32)  36.5 us
    psum x1, waiting for transfers between devices, body(): lax.psum(lax.dot_general(grad_pre_low, w_in, contract_last, preferred_ele...  27.2 us
    psum x1, waiting for transfers between devices, body(): lax.psum(mlp_partial.astype(jnp.bfloat16), 'tensor').astype(jnp.float32)  24.1 us
    unnamed x108, local copies, waits for them, and re-layouts  14.3 us
  transfers between devices with their start and end apart: 7, of which 6 were waited for; matrix products, arithmetic and copies ran while one was open for 8% of the time, Pallas kernels for 0%

commit v1 on v0

v1 whole, which is shorter than its diff:
```python
import functools

import jax
import jax.numpy as jnp
from jax import lax
from jax.experimental import pallas as pl
from jax.experimental.pallas import tpu as pltpu
from jax.sharding import PartitionSpec as P

MESH = pl.DeviceIdType.MESH
BF = jnp.bfloat16
F32 = jnp.float32
HEAD = 64
NORM_EPS = 1e-06
MASKED = -1000000000.0
BITS = 4
WAYS = 2**BITS
CHUNK = 64
TILE = 384

NN = ((1,), (0,))
NT = ((1,), (1,))
TN = ((0,), (0,))


def dot(a, b, dims):
    return lax.dot_general(a, b, (dims, ((), ())), preferred_element_type=F32)


def loop(count, step):
    def run(i, carry):
        step(i)
        return carry

    lax.fori_loop(0, count, run, 0)


def cols(i, width):
    return pl.ds(pl.multiple_of(i * width, width), width)


def rows(i, height):
    return pl.ds(pl.multiple_of(i * height, height), height)


def kernel(
    stride,
    tok_h,
    seg_ref,
    wqkv_h,
    wout_h,
    win_h,
    wdn_h,
    vin,
    dy_h,
    block_h,
    gtok_h,
    gqkv_ref,
    gout_ref,
    gin_ref,
    gdn_ref,
    vout,
    tok,
    dy,
    wq,
    wo,
    win,
    wdn,
    a_buf,
    xh1,
    r1,
    qkv,
    p_buf,
    o_buf,
    h_buf,
    xh2,
    r2,
    c_buf,
    g_buf,
    du_buf,
    dc_snd,
    dc_rcv,
    mlp_snd,
    mlp_rcv,
    da_snd,
    da_rcv,
    do_buf,
    dhb,
    dp_buf,
    out_buf,
    l_t,
    grads,
    r0_buf,
    r1_buf,
    r2_buf,
    r3_buf,
    vacc,
    vrcv,
    in_sem,
    wo_send,
    wo_recv,
    x_send,
    x_recv,
    g_send,
    g_recv,
    v_send,
    v_recv,
    out_sem,
):
    d = lax.axis_index("dp")
    t = lax.axis_index("tensor")
    group = d // stride
    bit = [lax.rem(group // (2**b), 2) for b in range(BITS)]
    mate = [d + (1 - 2 * bit[b]) * (2**b) * stride for b in range(BITS)]
    seqs, length, width = 2, 256, tok.shape[-1]
    half = wo.shape[1] // 2
    pairs = wo.shape[2] // (2 * HEAD)
    hidden = win.shape[1]
    scale = HEAD ** (-0.5)

    loads = []

    def load(src, dst):
        copy = pltpu.make_async_copy(src, dst, in_sem.at[len(loads)])
        copy.start()
        loads.append(copy)
        return copy

    tok_load = load(tok_h, tok)
    wq_loads = [
        load(
            wqkv_h.at[kind, :, p * 128 : (p + 1) * 128],
            wq.at[:, p * 384 + kind * 128 : p * 384 + (kind + 1) * 128],
        )
        for p in range(pairs)
        for kind in range(3)
    ]
    wo_load = load(wout_h, wo.at[t])
    win_load = load(win_h, win)
    wdn_load = load(wdn_h, wdn)
    dy_load = load(dy_h, dy)

    barrier = pltpu.get_barrier_semaphore()
    pl.semaphore_signal(barrier, inc=1, device_id=(d, 1 - t), device_id_type=MESH)
    for b in range(BITS):
        pl.semaphore_signal(barrier, inc=1, device_id=(mate[b], t), device_id_type=MESH)
    pl.semaphore_wait(barrier, BITS + 1)

    def across(src, dst, send, recv):
        return pltpu.make_async_remote_copy(
            src_ref=src,
            dst_ref=dst,
            send_sem=send,
            recv_sem=recv,
            device_id=(d, 1 - t),
            device_id_type=MESH,
        )

    def toward(b, src, dst, send, recv):
        return pltpu.make_async_remote_copy(
            src_ref=src,
            dst_ref=dst,
            send_sem=send,
            recv_sem=recv,
            device_id=(mate[b], t),
            device_id_type=MESH,
        )

    part = pl.ds(pl.multiple_of(bit[0] * half, half), half)
    wo_first = across(wout_h.at[part], wo.at[t, part], wo_send.at[0], wo_recv.at[0])
    wo_second = toward(
        0, wo.at[1 - t, part], wo.at[1 - t, part], wo_send.at[1], wo_recv.at[1]
    )
    wo_first.start()

    def o_copy(s):
        return across(
            o_buf.at[t, rows(s, length)],
            o_buf.at[t, rows(s, length)],
            x_send.at[0, s],
            x_recv.at[0, s],
        )

    def x_copy(kind, snd, rcv, s):
        here = rows(s, length)
        return across(snd.at[here], rcv.at[here], x_send.at[kind, s], x_recv.at[kind, s])

    def dc_copy(s):
        return x_copy(1, dc_snd, dc_rcv, s)

    def mlp_copy(s):
        return x_copy(2, mlp_snd, mlp_rcv, s)

    def da_copy(s):
        return x_copy(3, da_snd, da_rcv, s)

    vacc[...] = jnp.zeros_like(vacc)

    lane = lax.broadcasted_iota(jnp.int32, (1, 128), 1)
    low_half = lane < HEAD

    def stacked(value):
        zero = jnp.zeros_like(value)
        return jnp.concatenate(
            [jnp.where(low_half, value, zero), jnp.where(low_half, zero, value)], axis=0
        )

    def normalize(value):
        mean = jnp.sum(value, axis=-1, keepdims=True) * (1.0 / width)
        center = value - mean
        spread = jnp.sum(center * center, axis=-1, keepdims=True) * (1.0 / width)
        scale_back = lax.rsqrt(spread + NORM_EPS)
        return center * scale_back, scale_back

    def norm_back(grad, normed, scale_back, gain):
        inner = grad * gain
        mean_one = jnp.sum(inner, axis=-1, keepdims=True) * (1.0 / width)
        mean_two = jnp.sum(inner * normed, axis=-1, keepdims=True) * (1.0 / width)
        return scale_back * (inner - mean_one - normed * mean_two)

    def same_image(s):
        ids = jnp.where(s == 0, seg_ref[0:1], seg_ref[1:2]).astype(F32)
        down = jnp.broadcast_to(ids, (128, length)).T
        return jnp.concatenate(
            [down == ids[:, i * 128 : (i + 1) * 128] for i in range(length // 128)], axis=1
        )

    tok_load.wait()
    for copy in wq_loads:
        copy.wait()

    def forward_one(s):
        def norm_step(i):
            here = rows(s * (length // CHUNK) + i, CHUNK)
            normed, scale_back = normalize(tok[here].astype(F32))
            xh1[here] = normed
            r1[here] = scale_back
            a_buf[here] = (normed * vin[0:1] + vin[2:3]).astype(BF)

        loop(length // CHUNK, norm_step)
        seq = rows(s, length)
        allowed = same_image(s)

        def pair_step(p):
            bias = jnp.concatenate(
                [
                    vin[8:9, cols(p, 128)],
                    jnp.zeros((1, 128), F32),
                    vin[8:9, pl.ds(pl.multiple_of(pairs * 128 + p * 128, 128), 128)],
                ],
                axis=1,
            )
            mixed = (dot(a_buf[seq], wq[:, cols(p, 384)], NN) + bias).astype(BF)
            qkv[seq, cols(p, 384)] = mixed
            scores = dot(mixed[:, :128], stacked(mixed[:, 128:256]), NT) * scale
            soft = []
            for e in range(2):
                one = jnp.where(allowed, scores[:, e * length : (e + 1) * length], MASKED)
                expo = jnp.exp(one - jnp.max(one, axis=-1, keepdims=True))
                soft.append(expo * (1.0 / jnp.sum(expo, axis=-1, keepdims=True)))
            both = jnp.concatenate(soft, axis=1)
            p_buf[s * pairs + p] = both
            o_buf[t, seq, cols(p, 128)] = dot(
                both.astype(BF), stacked(mixed[:, 256:]), NN
            ).astype(BF)

        loop(pairs, pair_step)
        o_copy(s).start()

    loop(seqs, forward_one)

    wo_first.wait_recv()
    wo_second.start()
    wo_load.wait()
    win_load.wait()
    wdn_load.wait()
    dy_load.wait()
    wo_second.wait_recv()

    def middle_one(s):
        seq = rows(s, length)
        o_copy(s).wait_recv()
        h_buf[seq] = dot(o_buf[0, seq], wo[0], NT) + dot(o_buf[1, seq], wo[1], NT)

        def norm_step(i):
            here = rows(s * (length // CHUNK) + i, CHUNK)
            resid = h_buf[here] + vin[4:5] + tok[here].astype(F32)
            h_buf[here] = resid
            normed, scale_back = normalize(resid)
            xh2[here] = normed
            r2[here] = scale_back
            c_buf[here] = (normed * vin[1:2] + vin[3:4]).astype(BF)

        loop(length // CHUNK, norm_step)

        for n in range(2):
            size = hidden // 2

            def hidden_step(i, n=n, size=size):
                here = pl.ds(pl.multiple_of(n * size + i * 256, 256), 256)
                there = cols(i, 256)
                pre = dot(c_buf[seq], win[:, here], NN) + vin[6 + n : 7 + n, there]
                back = dot(dy[seq], wdn[:, here], NN)
                phi = 0.5 + 0.5 * lax.erf(pre * 0.7071067811865476)
                g_buf[seq, here] = (pre * phi).astype(BF)
                slope = phi + pre * (jnp.exp(-0.5 * pre * pre) * 0.3989422804014327)
                low = (back * slope).astype(BF)
                du_buf[seq, here] = low
                vacc[1 + n : 2 + n, there] += jnp.sum(low.astype(F32), axis=0, keepdims=True)

            loop(size // 256, hidden_step)

        def back_step(i):
            here = cols(i, 256)
            grad = dot(du_buf[seq], win[rows(i, 256)], NT)
            dc_snd[seq, here] = grad.astype(BF)
            vacc[6:7, here] += jnp.sum(grad * xh2[seq, here], axis=0, keepdims=True)
            vacc[8:9, here] += jnp.sum(grad, axis=0, keepdims=True)

        loop(width // 256, back_step)
        dc_copy(s).start()

    loop(seqs, middle_one)

    def turn(src):
        for s in range(seqs):
            l_t[:, s * length : (s + 1) * length] = src[s * length : (s + 1) * length].T

    strip = width // WAYS

    def product(piece, right):
        full = dot(l_t[...], right, NN)
        for k in range(WAYS):
            b = [(k >> i) & 1 for i in range(BITS)]
            grads[piece, b[0], b[1], b[2], b[3]] = full[k * strip : (k + 1) * strip].astype(BF)

    received = [r0_buf, r1_buf, r2_buf, r3_buf]

    def own(piece, depth):
        return (piece,) + tuple(bit[:depth])

    def g_copy(piece, k):
        return toward(
            k,
            grads.at[own(piece, k) + (1 - bit[k],)],
            received[k].at[piece],
            g_send.at[piece, k],
            g_recv.at[piece, k],
        )

    def pass_on(piece, k):
        g_copy(piece, k).wait_recv()
        here = own(piece, k + 1)
        grads[here] = (grads[here].astype(F32) + received[k][piece].astype(F32)).astype(BF)
        g_copy(piece, k + 1).start()

    def finish(piece):
        g_copy(piece, 3).wait_recv()
        return grads[own(piece, 4)].astype(F32) + received[3][piece].astype(F32)

    hidden_pieces = hidden // TILE
    down, into, outs, mixes = 0, hidden_pieces, 2 * hidden_pieces, 2 * hidden_pieces + 1
    total = mixes + pairs

    turn(dy)

    def down_step(i):
        product(down + i, g_buf[:, cols(i, TILE)])
        g_copy(down + i, 0).start()

    loop(hidden_pieces, down_step)
    vacc[4:5] += jnp.sum(dy[...].astype(F32), axis=0, keepdims=True)

    def mlp_out(s):
        seq = rows(s, length)

        def step(i):
            mlp_snd[seq, cols(i, 256)] = dot(g_buf[seq], wdn[rows(i, 256)], NT).astype(BF)

        loop(width // 256, step)
        mlp_copy(s).start()

    def resid_back(s):
        seq = rows(s, length)
        dc_copy(s).wait_recv()

        def step(i):
            here = rows(s * (length // CHUNK) + i, CHUNK)
            grad = dc_snd[here].astype(F32) + dc_rcv[here].astype(F32)
            full = dy[here].astype(F32) + norm_back(grad, xh2[here], r2[here], vin[1:2])
            xh2[here] = full
            dhb[here] = full.astype(BF)
            vacc[3:4] += jnp.sum(full, axis=0, keepdims=True)

        loop(length // CHUNK, step)
        do_buf[seq] = dot(dhb[seq], wo[t], NN).astype(BF)

    def attention_back(s, p):
        seq = rows(s, length)
        mixed = qkv[seq, cols(p, 384)]
        query, keys = mixed[:, :128], stacked(mixed[:, 128:256])
        grad_o = do_buf[seq, cols(p, 128)]
        soft = p_buf[s * pairs + p]
        grad_soft = dot(grad_o, stacked(mixed[:, 256:]), NT)
        parts = []
        for e in range(2):
            one, two = (v[:, e * length : (e + 1) * length] for v in (soft, grad_soft))
            delta = jnp.sum(one * two, axis=-1, keepdims=True)
            parts.append((one * (two - delta)).astype(BF))
        grad_scores = jnp.concatenate(parts, axis=1)
        grad_query = dot(grad_scores, keys, NN) * scale
        grad_keys = dot(grad_scores, query, TN) * scale
        grad_keys = jnp.where(low_half, grad_keys[:length], grad_keys[length:])
        grad_values = dot(soft.astype(BF), grad_o, TN)
        grad_values = jnp.where(low_half, grad_values[:length], grad_values[length:])
        low = [v.astype(BF) for v in (grad_query, grad_keys, grad_values)]
        dp_buf[seq, cols(p, 384)] = jnp.concatenate(low, axis=1)
        vacc[0:1, cols(p, 128)] += jnp.sum(low[0].astype(F32), axis=0, keepdims=True)
        vacc[0:1, pl.ds(pl.multiple_of(pairs * 128 + p * 128, 128), 128)] += jnp.sum(
            low[2].astype(F32), axis=0, keepdims=True
        )

    def mixed_back(s):
        seq = rows(s, length)

        def step(i):
            here = cols(i, 256)
            grad = dot(dp_buf[seq], wq[rows(i, 256)], NT)
            da_snd[seq, here] = grad.astype(BF)
            vacc[5:6, here] += jnp.sum(grad * xh1[seq, here], axis=0, keepdims=True)
            vacc[7:8, here] += jnp.sum(grad, axis=0, keepdims=True)

        loop(width // 256, step)
        da_copy(s).start()

    resid_back(0)
    loop(hidden_pieces, lambda i: pass_on(down + i, 0))
    mlp_out(0)
    loop(pairs, lambda p: attention_back(0, p))
    mixed_back(0)

    turn(c_buf)

    def into_step(i):
        product(into + i, du_buf[:, cols(i, TILE)])
        g_copy(into + i, 0).start()

    loop(hidden_pieces, into_step)
    loop(hidden_pieces, lambda i: pass_on(down + i, 1))

    resid_back(1)
    loop(hidden_pieces, lambda i: pass_on(into + i, 0))
    turn(dhb)
    product(outs, o_buf[t])
    g_copy(outs, 0).start()
    loop(hidden_pieces, lambda i: pass_on(down + i, 2))

    turn(a_buf)

    def last_step(p):
        attention_back(1, p)
        product(mixes + p, dp_buf[:, cols(p, 384)])
        g_copy(mixes + p, 0).start()

    loop(pairs, last_step)
    mixed_back(1)
    pass_on(outs, 0)
    loop(pairs, lambda p: pass_on(mixes + p, 0))
    mlp_out(1)

    def v_copy(k):
        if k == BITS:
            return across(vacc_at(k), vrcv.at[k], v_send.at[k], v_recv.at[k])
        return toward(k, vacc_at(k), vrcv.at[k], v_send.at[k], v_recv.at[k])

    def vacc_at(k):
        return vsum.at[k]

    vsum = vout.at[1:]
    vsum[0] = vacc[...]
    v_copy(0).start()

    def v_next(k):
        v_copy(k).wait_recv()
        vsum[k + 1] = vsum[k] + vrcv[k]
        v_copy(k + 1).start()

    loop(hidden_pieces, lambda i: pass_on(into + i, 1))
    v_next(0)
    loop(hidden_pieces, lambda i: pass_on(into + i, 2))

    def down_out(i):
        gdn_ref[:, cols(i, TILE)] = finish(down + i)

    def into_out(i):
        gin_ref[:, cols(i, TILE)] = finish(into + i)

    loop(hidden_pieces, down_out)
    pass_on(outs, 1)
    v_next(1)

    def finish_block(s):
        mlp_copy(s).wait_recv()

        def step(i):
            here = rows(s * (length // CHUNK) + i, CHUNK)
            added = mlp_snd[here].astype(F32) + mlp_rcv[here].astype(F32)
            out_buf[0, here] = (h_buf[here] + (added + vin[5:6])).astype(BF)

        loop(length // CHUNK, step)
        out_copy(0, block_h, s).start()

    def out_copy(n, dst, s):
        here = rows(s, length)
        return pltpu.make_async_copy(out_buf.at[n, here], dst.at[here], out_sem.at[n, s])

    def finish_tokens(s):
        da_copy(s).wait_recv()

        def step(i):
            here = rows(s * (length // CHUNK) + i, CHUNK)
            grad = da_snd[here].astype(F32) + da_rcv[here].astype(F32)
            full = xh2[here] + norm_back(grad, xh1[here], r1[here], vin[0:1])
            out_buf[1, here] = full.astype(BF)

        loop(length // CHUNK, step)
        out_copy(1, gtok_h, s).start()

    finish_block(0)
    finish_tokens(0)
    loop(pairs, lambda p: pass_on(mixes + p, 1))
    v_next(2)
    pass_on(outs, 2)
    loop(hidden_pieces, into_out)
    loop(pairs, lambda p: pass_on(mixes + p, 2))
    v_next(3)
    gout_ref[...] = finish(outs)
    finish_tokens(1)
    finish_block(1)

    def mix_out(p):
        value = finish(mixes + p)
        for kind in range(3):
            gqkv_ref[kind, :, cols(p, 128)] = value[:, kind * 128 : (kind + 1) * 128]

    loop(pairs, mix_out)

    v_copy(BITS).wait_recv()
    line = lax.broadcasted_iota(jnp.int32, vacc.shape, 0)
    norms = (line >= 5) & (line < 9)
    final = vsum[BITS]
    vout[0] = jnp.where(norms, final + vrcv[BITS], final)

    wo_first.wait_send()
    wo_second.wait_send()
    for s in range(seqs):
        o_copy(s).wait_send()
        dc_copy(s).wait_send()
        mlp_copy(s).wait_send()
        da_copy(s).wait_send()
        out_copy(0, block_h, s).wait()
        out_copy(1, gtok_h, s).wait()

    def sent(i):
        for k in range(BITS):
            g_copy(i, k).wait_send()

    loop(total, sent)
    for k in range(BITS + 1):
        v_copy(k).wait_send()


def body(
    tokens,
    segment_ids,
    w_qkv,
    qv_bias,
    w_out,
    out_bias,
    w_in,
    hidden_bias,
    w_down,
    mlp_bias,
    ln_gain,
    ln_bias,
    cotangent,
    *,
    dp,
):
    seqs, length, width = tokens.shape
    count = seqs * length
    local = w_qkv.shape[2]
    hidden = w_in.shape[1]
    pairs = local // (2 * HEAD)
    stride = dp // WAYS
    strip = width // WAYS
    pieces = 2 * (hidden // TILE) + 1 + pairs
    lines = jnp.concatenate(
        [
            ln_gain.astype(F32),
            ln_bias.astype(F32),
            out_bias.astype(F32)[None],
            mlp_bias.astype(F32)[None],
            hidden_bias.astype(F32).reshape(2, width),
            qv_bias.astype(F32).reshape(1, width),
            jnp.zeros((7, width), F32),
        ],
        axis=0,
    )
    hbm = pl.BlockSpec(memory_space=pl.ANY)
    vmem = pl.BlockSpec(memory_space=pltpu.VMEM)
    dma = pltpu.SemaphoreType.DMA
    wide = (count, width)
    outs = pl.pallas_call(
        functools.partial(kernel, stride),
        out_shape=(
            jax.ShapeDtypeStruct(wide, BF),
            jax.ShapeDtypeStruct(wide, BF),
            jax.ShapeDtypeStruct((3, strip, local), F32),
            jax.ShapeDtypeStruct((strip, local), F32),
            jax.ShapeDtypeStruct((strip, hidden), F32),
            jax.ShapeDtypeStruct((strip, hidden), F32),
            jax.ShapeDtypeStruct((BITS + 2, 16, width), F32),
        ),
        in_specs=[hbm, vmem, hbm, hbm, hbm, hbm, vmem, hbm],
        out_specs=(hbm, hbm, vmem, vmem, vmem, vmem, vmem),
        scratch_shapes=[
            pltpu.VMEM(wide, BF),
            pltpu.VMEM(wide, BF),
            pltpu.VMEM((width, 3 * local), BF),
            pltpu.VMEM((2, width, local), BF),
            pltpu.VMEM((width, hidden), BF),
            pltpu.VMEM((width, hidden), BF),
            pltpu.VMEM(wide, BF),
            pltpu.VMEM(wide, F32),
            pltpu.VMEM((count, 1), F32),
            pltpu.VMEM((count, 3 * local), BF),
            pltpu.VMEM((seqs * pairs, length, 2 * length), F32),
            pltpu.VMEM((2, count, local), BF),
            pltpu.VMEM(wide, F32),
            pltpu.VMEM(wide, F32),
            pltpu.VMEM((count, 1), F32),
            pltpu.VMEM(wide, BF),
            pltpu.VMEM((count, hidden), BF),
            pltpu.VMEM((count, hidden), BF),
            pltpu.VMEM(wide, BF),
            pltpu.VMEM(wide, BF),
            pltpu.VMEM(wide, BF),
            pltpu.VMEM(wide, BF),
            pltpu.VMEM(wide, BF),
            pltpu.VMEM(wide, BF),
            pltpu.VMEM((count, local), BF),
            pltpu.VMEM(wide, BF),
            pltpu.VMEM((count, 3 * local), BF),
            pltpu.VMEM((2, count, width), BF),
            pltpu.VMEM((width, count), BF),
            pltpu.VMEM((pieces, 2, 2, 2, 2, strip, TILE), BF),
            pltpu.VMEM((pieces, 2, 2, 2, strip, TILE), BF),
            pltpu.VMEM((pieces, 2, 2, strip, TILE), BF),
            pltpu.VMEM((pieces, 2, strip, TILE), BF),
            pltpu.VMEM((pieces, strip, TILE), BF),
            pltpu.VMEM((16, width), F32),
            pltpu.VMEM((BITS + 1, 16, width), F32),
            dma((5 + 3 * pairs,)),
            dma((2,)),
            dma((2,)),
            dma((4, seqs)),
            dma((4, seqs)),
            dma((pieces, BITS)),
            dma((pieces, BITS)),
            dma((BITS + 1,)),
            dma((BITS + 1,)),
            dma((2, seqs)),
        ],
        compiler_params=pltpu.CompilerParams(
            collective_id=0, has_side_effects=True, vmem_limit_bytes=60 * 2**20
        ),
        cost_estimate=pl.CostEstimate(
            flops=12 * 10**9, bytes_accessed=12 * 10**6, transcendentals=4 * 10**6
        ),
    )(
        tokens.reshape(wide),
        segment_ids,
        w_qkv.transpose(1, 0, 2),
        w_out,
        w_in,
        w_down,
        lines,
        cotangent.reshape(wide),
    )
    block, grad_tokens, gqkv, gout, gin, gdn, small = outs
    small = small[0]
    gqkv = gqkv.transpose(1, 0, 2)
    if stride > 1:
        groups = [[g * stride + i for i in range(stride)] for g in range(WAYS)]
        gqkv, gout, gin, gdn = (
            lax.psum_scatter(v, "dp", scatter_dimension=0, axis_index_groups=groups, tiled=True)
            for v in (gqkv, gout, gin, gdn)
        )
        small = lax.psum(small, "dp", axis_index_groups=groups)
    return (
        block.reshape(tokens.shape),
        grad_tokens.reshape(tokens.shape),
        gqkv,
        small[0].reshape(2, local),
        gout,
        small[3],
        gin,
        small[1:3].reshape(hidden),
        gdn,
        small[4],
        small[5:7],
        small[7:9],
    )


def solution(mesh):
    return jax.shard_map(
        functools.partial(body, dp=mesh.shape["dp"]),
        mesh=mesh,
        in_specs=(
            P("dp", None, None),
            P("dp", None),
            P(None, None, "tensor"),
            P(None, "tensor"),
            P(None, "tensor"),
            P(),
            P(None, "tensor"),
            P("tensor"),
            P(None, "tensor"),
            P(),
            P(),
            P(),
            P("dp", None, None),
        ),
        out_specs=(
            P("dp", None, None),
            P("dp", None, None),
            P("dp", None, "tensor"),
            P(None, "tensor"),
            P("dp", "tensor"),
            P(),
            P("dp", "tensor"),
            P("tensor"),
            P("dp", "tensor"),
            P(),
            P(),
            P(),
        ),
        check_vma=False,
    )
```

time: 509 us -> 103 us (0.20)
  waiting for transfers between devices: 311 us -> 0 us
  Pallas kernels: 0 us -> 86.5 us
  blocking collectives: 61.9 us -> 0 us
  matrix products: 50.9 us -> 0 us
  other arithmetic: 29.7 us -> 0.68 us
  local copies, waits for them, and re-layouts: 38.8 us -> 15.1 us
  between operations: 14.8 us -> 0.69 us
    reduce_scatter x3 -> x0, waiting for transfers between devices: 144 us -> none  [the longest x1 79.2 us: body(): lax.psum_scatter(grad_in, 'dp', scatter_dimension=0, tiled=True)]
    psum x3 -> x0, waiting for transfers between devices: 87.7 us -> none  [the longest x1 36.5 us: body(): lax.psum(attn_partial.astype(jnp.bfloat16), 'tensor').astype(jnp.float32)]
    pallas_call x0 -> x1, Pallas kernels: none -> 86.5 us  [body(): pl.pallas_call(functools.partial(kernel, stride), out_shape=(jax.ShapeDty...]
    unnamed x8 -> x0, waiting for transfers between devices: 79.2 us -> none
    psum x1 -> x0, blocking collectives: 61.9 us -> none  [body(): lax.psum((grad_bias_pair, grad_out_bias, grad_hidden_bias, grad_mlp_bias,...]
    dot_general x18 -> x0, matrix products: 50.9 us -> none  [the longest x1 10.1 us: body(): grad_active = jnp.dot(grad_low, w_down, preferred_element_type=jnp.float32)]
    reduce_sum x11 -> x0, other arithmetic: 17 us -> none  [the longest x4 7.9 us: layer_norm(): return center * lax.rsqrt(spread + norm_eps) * gain + shift]
    convert_element_type x12 -> x0, local copies, waits for them, and re-layouts: 14.1 us -> none  [the longest x3 5.07 us: body(): grad_values.reshape(row_count, local_width).astype(jnp.bfloat16)]
  transfers between devices with their start and end apart: 7 -> 0, of which waited for: 6 -> 0; matrix products, arithmetic and copies ran while one was open for 8% -> 0% of each run, Pallas kernels for 0% -> 0%
where the time goes in v1:
time: 103 us
  Pallas kernels  86.5 us (84%)
  local copies, waits for them, and re-layouts  15.1 us (15%)
    pallas_call x1, Pallas kernels, body(): pl.pallas_call(functools.partial(kernel, stride), out_shape=(jax.ShapeDty...  86.5 us
    unnamed x15, local copies, waits for them, and re-layouts  6.89 us

profile of v1, /device:TPU:0, one launch (start us, length us, event | category | flops | bytes accessed | tf_op | source)
XLA Modules:
  0.0 103.0 jit_solution(15815749261620405878)
XLA Ops:
  0.6 0.7 convert_bitcast_fusion
  1.3 0.7 reshape.73
  2.0 0.7 reshape.70
  2.7 0.7 reshape.71
  3.4 2.0 %concatenate.3.vin = f32[16,768]{1,0:T(8,128)} concatenate(bf16[2,768]{1,0:T(2,128)(2,1)} %param.23, bf16[2,768]{1,0:T(2,128)(2,1)} %param.24, f32[1,768]{1,0:T(1,128)S(1)} %reshape.70, f32[1,768]{1,0:T(1,128)S(1)} %reshape.71, f32[2,768]{1,0:T(2,128)S(1)} %reshape.73, f32[1,768]{1,0:T(1,128)S(1)} %bitcast.17, f32[7,768]{1,0:T(8,128)S(1)} %broadcast_in_dim.19), dimensions={0} | concatenate | bytes 92160 | tf_op jit(solution)/shard_map/concatenate | solution.py:598
  5.4 86.5 %shard_map.220 = (bf16[512,768]{1,0:T(8,128)(2,1)}, bf16[512,768]{1,0:T(8,128)(2,1)}, f32[3,48,384]{2,1,0:T(8,128)}, f32[48,384]{1,0:T(8,128)}, f32[48,1536]{1,0...) custom-call(bf16[512,768]{1,0:T(8,128)(2,1)} %bitcast.19, s32[2,256]{1,0:T(2,128)} %seg_ref.1, ...), custom_call_target="tpu_custom_call" | custom-call | flops 12000000000 | bytes 12000000 | tf_op jit(solution)/shard_map/pallas_call | solution.py:614
  91.9 0.0 copy-start.2
  91.9 0.0 copy-start.3
  91.9 0.0 copy-start.1
  91.9 0.0 copy-start
  91.9 1.5 %slice_bitcast_fusion = (f32[2,768]{1,0:T(2,128)}, f32[1,2,768]{2,1,0:T(2,128)S(1)}, f32[2,768]{1,0:T(2,128)}) fusion(f32[6,16,768]{2,1,0:T(8,128)} %get-tuple-element.22), kind=kLoop, calls=%fused_computation | loop fusion | bytes 36864 | tf_op jit(solution)/shard_map/slice | solution.py:713
  93.4 0.6 reshape.69
  94.0 1.5 %slice_reduce_fusion = (f32[768]{0:T(1024)}, f32[768]{0:T(1024)}, f32[768]{0:T(1024)S(1)}) fusion(f32[6,16,768]{2,1,0:T(8,128)} %get-tuple-element.22), kind=kLoop, calls=%fused_computation.3 | loop fusion | bytes 18432 | tf_op jit(solution)/shard_map/slice | solution.py:711
  95.5 0.6 reshape_squeeze.3
  96.1 2.1 %copy.32 = bf16[2,256,768]{2,1,0:T(8,128)(2,1)} copy(bf16[2,256,768]{2,1,0:T(8,128)(2,1)} %bitcast.15) | data formatting | bytes 1572864
  98.2 2.1 %copy.33 = bf16[2,256,768]{2,1,0:T(8,128)(2,1)} copy(bf16[2,256,768]{2,1,0:T(8,128)(2,1)} %bitcast.14) | data formatting | bytes 1572864
  100.2 0.0 copy-done.2
  100.2 0.7 copy.34
  100.9 0.0 copy-done.3
  100.9 0.6 copy.35
  101.5 0.0 copy-done.1
  101.5 0.7 copy.36
  102.3 0.0 copy-done
  102.3 0.7 copy.37
  (2 shorter events, 0.0 us)
Async XLA Ops:
  91.9 8.3 %copy-start.2 = (f32[3,48,384]{2,1,0:T(8,128)S(1)}, f32[3,48,384]{2,1,0:T(8,128)}, u32[]{:S(2)}) copy-start(f32[3,48,384]{2,1,0:T(8,128)} %get-tuple-element.21) | copy-start | bytes 663556
  91.9 9.0 %copy-start.3 = (f32[48,384]{1,0:T(8,128)S(1)}, f32[48,384]{1,0:T(8,128)}, u32[]{:S(2)}) copy-start(f32[48,384]{1,0:T(8,128)} %get-tuple-element.48) | copy-start | bytes 221188
  91.9 9.6 %copy-start.1 = (f32[48,1536]{1,0:T(8,128)S(1)}, f32[48,1536]{1,0:T(8,128)}, u32[]{:S(2)}) copy-start(f32[48,1536]{1,0:T(8,128)} %get-tuple-element.50) | copy-start | bytes 884740
  91.9 10.3 %copy-start = (f32[48,1536]{1,0:T(8,128)S(1)}, f32[48,1536]{1,0:T(8,128)}, u32[]{:S(2)}) copy-start(f32[48,1536]{1,0:T(8,128)} %get-tuple-element.52) | copy-start | bytes 884740

commit v2 on v1

v2 whole, which is shorter than its diff:
```python
import functools

import jax
import jax.numpy as jnp
from jax import lax
from jax.experimental import pallas as pl
from jax.experimental.pallas import tpu as pltpu
from jax.sharding import PartitionSpec as P

MESH = pl.DeviceIdType.MESH
BF = jnp.bfloat16
F32 = jnp.float32
HEAD = 64
NORM_EPS = 1e-06
MASKED = -1000000000.0
BITS = 4
WAYS = 2**BITS
BLOCK = 256
CHUNK = 64
TILE = 384

NN = ((1,), (0,))
NT = ((1,), (1,))
TN = ((0,), (0,))


def dot(a, b, dims):
    return lax.dot_general(a, b, (dims, ((), ())), preferred_element_type=F32)


def loop(count, step):
    def run(i, carry):
        step(i)
        return carry

    lax.fori_loop(0, count, run, 0)


def cols(i, width):
    return pl.ds(pl.multiple_of(i * width, width), width)


def rows(i, height):
    return pl.ds(pl.multiple_of(i * height, height), height)


def kernel(
    stride,
    tok_h,
    seg_ref,
    wqkv_h,
    qvb_ref,
    wout_h,
    ob_ref,
    win_h,
    hb_ref,
    wdn_h,
    mb_ref,
    gain_ref,
    shift_ref,
    dy_h,
    block_h,
    gtok_h,
    gqkv_ref,
    gout_ref,
    gin_ref,
    gdn_ref,
    vout,
    tok,
    dy,
    wq,
    wo,
    win,
    wdn,
    vin,
    a_buf,
    xh1,
    r1,
    qkv,
    p_buf,
    o_buf,
    h_buf,
    xh2,
    r2,
    c_buf,
    g_buf,
    du_buf,
    dc_snd,
    dc_rcv,
    mlp_snd,
    mlp_rcv,
    da_snd,
    da_rcv,
    do_buf,
    dhb,
    dp_buf,
    out_buf,
    l_t,
    grads,
    r0_buf,
    r1_buf,
    r2_buf,
    r3_buf,
    vsum,
    vrcv,
    in_sem,
    wo_send,
    wo_recv,
    o_send,
    o_recv,
    x_send,
    x_recv,
    g_send,
    g_recv,
    v_send,
    v_recv,
    out_sem,
):
    d = lax.axis_index("dp")
    t = lax.axis_index("tensor")
    group = d // stride
    bit = [lax.rem(group // (2**b), 2) for b in range(BITS)]
    mate = [d + (1 - 2 * bit[b]) * (2**b) * stride for b in range(BITS)]
    count, width = tok.shape
    seqs = seg_ref.shape[0]
    length = count // seqs
    local = wo.shape[2]
    pairs = local // (2 * HEAD)
    hidden = win.shape[1]
    scale = HEAD ** (-0.5)
    blocks = count // BLOCK
    vacc = vsum.at[0]

    barrier = pltpu.get_barrier_semaphore()
    pl.semaphore_signal(barrier, inc=1, device_id=(d, 1 - t), device_id_type=MESH)
    for b in range(BITS):
        pl.semaphore_signal(barrier, inc=1, device_id=(mate[b], t), device_id_type=MESH)

    loads = []

    def load(src, dst):
        copy = pltpu.make_async_copy(src, dst, in_sem.at[len(loads)])
        copy.start()
        loads.append(copy)
        return copy

    tok_load = load(tok_h, tok)
    wq_loads = [
        load(
            wqkv_h.at[kind, :, p * 128 : (p + 1) * 128],
            wq.at[:, p * 384 + kind * 128 : p * 384 + (kind + 1) * 128],
        )
        for p in range(pairs)
        for kind in range(3)
    ]
    dy_load = load(dy_h, dy)
    wo_load = load(wout_h, wo.at[t])
    win_load = load(win_h, win)
    wdn_load = load(wdn_h, wdn)

    def across(src, dst, send, recv):
        return pltpu.make_async_remote_copy(
            src_ref=src,
            dst_ref=dst,
            send_sem=send,
            recv_sem=recv,
            device_id=(d, 1 - t),
            device_id_type=MESH,
        )

    def toward(b, src, dst, send, recv):
        return pltpu.make_async_remote_copy(
            src_ref=src,
            dst_ref=dst,
            send_sem=send,
            recv_sem=recv,
            device_id=(mate[b], t),
            device_id_type=MESH,
        )

    slab = width // 8

    def wo_rows(turned, part):
        first = bit[0]
        second = 1 - bit[1] if turned else bit[1]
        return rows((2 * second + first) * 2 + part, slab)

    def wo_copy(step, part):
        sems = wo_send.at[step, part], wo_recv.at[step, part]
        if step == 0:
            here = wo_rows(False, part)
            return across(wout_h.at[here], wo.at[t, here], *sems)
        here = wo_rows(step == 3, part)
        return toward(1 if step == 2 else 0, wo.at[1 - t, here], wo.at[1 - t, here], *sems)

    def wo_share(part):
        wo_copy(0, part).wait_recv()
        wo_copy(2, part).start()
        wo_copy(1, part).start()

    def wo_forward(part):
        wo_copy(2, part).wait_recv()
        wo_copy(3, part).start()

    def o_copy(s, p):
        here = rows(s, length)
        place = o_buf.at[t, here, cols(p, 128)]
        return across(place, place, o_send.at[s, p], o_recv.at[s, p])

    def dc_copy(n, i):
        here = rows(n, BLOCK), cols(i, 256)
        return across(
            dc_snd.at[here], dc_rcv.at[here], x_send.at[0, n, i], x_recv.at[0, n, i]
        )

    def da_copy(s, i):
        here = rows(s, length), cols(i, 256)
        return across(
            da_snd.at[here], da_rcv.at[here], x_send.at[1, s, i], x_recv.at[1, s, i]
        )

    def mlp_copy(s, i):
        here = rows(s, length), cols(i, 256)
        return across(
            mlp_snd.at[here], mlp_rcv.at[here], x_send.at[2, s, i], x_recv.at[2, s, i]
        )

    wide = width // 256

    vacc[...] = jnp.zeros(vacc.shape, F32)
    vin[0:2] = gain_ref[...].astype(F32)
    vin[2:4] = shift_ref[...].astype(F32)
    vin[4:5] = ob_ref[...].astype(F32).reshape(1, width)
    vin[5:6] = mb_ref[...].astype(F32).reshape(1, width)
    line = hb_ref[...].astype(F32).reshape(1, hidden)
    vin[6:7] = line[:, :width]
    vin[7:8] = line[:, width:]
    vin[8:9, :local] = qvb_ref[0:1].astype(F32)
    vin[8:9, local:] = qvb_ref[1:2].astype(F32)

    lane = lax.broadcasted_iota(jnp.int32, (1, 128), 1)
    low_half = lane < HEAD

    def stacked(value):
        zero = jnp.zeros_like(value)
        return jnp.concatenate(
            [jnp.where(low_half, value, zero), jnp.where(low_half, zero, value)], axis=0
        )

    def normalize(value):
        mean = jnp.sum(value, axis=-1, keepdims=True) * (1.0 / width)
        center = value - mean
        spread = jnp.sum(center * center, axis=-1, keepdims=True) * (1.0 / width)
        scale_back = lax.rsqrt(spread + NORM_EPS)
        return center * scale_back, scale_back

    def norm_back(grad, normed, scale_back, gain):
        inner = grad * gain
        mean_one = jnp.sum(inner, axis=-1, keepdims=True) * (1.0 / width)
        mean_two = jnp.sum(inner * normed, axis=-1, keepdims=True) * (1.0 / width)
        return scale_back * (inner - mean_one - normed * mean_two)

    def same_image(s):
        ids = seg_ref[s : s + 1].astype(F32)
        down = jnp.broadcast_to(ids, (128, length)).T
        return jnp.concatenate(
            [down == ids[:, i * 128 : (i + 1) * 128] for i in range(length // 128)], axis=1
        )

    def norm_one(s):
        def step(i):
            here = rows(s * (length // CHUNK) + i, CHUNK)
            normed, scale_back = normalize(tok[here].astype(F32))
            xh1[here] = normed
            r1[here] = scale_back
            a_buf[here] = (normed * vin[0:1] + vin[2:3]).astype(BF)

        loop(length // CHUNK, step)

    def attention(s):
        seq = rows(s, length)
        allowed = same_image(s)

        def pair_step(p):
            bias = jnp.concatenate(
                [
                    vin[8:9, cols(p, 128)],
                    jnp.zeros((1, 128), F32),
                    vin[8:9, cols(pairs + p, 128)],
                ],
                axis=1,
            )
            mixed = (dot(a_buf[seq], wq[:, cols(p, 384)], NN) + bias).astype(BF)
            qkv[seq, cols(p, 384)] = mixed
            scores = dot(mixed[:, :128], stacked(mixed[:, 128:256]), NT) * scale
            soft = []
            for e in range(2):
                one = jnp.where(allowed, scores[:, e * length : (e + 1) * length], MASKED)
                expo = jnp.exp(one - jnp.max(one, axis=-1, keepdims=True))
                soft.append(expo * (1.0 / jnp.sum(expo, axis=-1, keepdims=True)))
            both = jnp.concatenate(soft, axis=1)
            p_buf[s * pairs + p] = both
            o_buf[t, seq, cols(p, 128)] = dot(
                both.astype(BF), stacked(mixed[:, 256:]), NN
            ).astype(BF)
            o_copy(s, p).start()

        loop(pairs, pair_step)

    tok_load.wait()
    norm_one(0)
    pl.semaphore_wait(barrier, BITS + 1)
    wo_copy(0, 0).start()
    wo_copy(0, 1).start()
    for copy in wq_loads:
        copy.wait()
    attention(0)
    wo_share(0)
    norm_one(1)
    wo_share(1)
    attention(1)

    def turn(src):
        for s in range(seqs):
            l_t[:, s * length : (s + 1) * length] = src[s * length : (s + 1) * length].T

    strip = width // WAYS
    received = [r0_buf, r1_buf, r2_buf, r3_buf]

    def product(piece, right, order):
        full = dot(l_t[...], right, NN)
        for k in range(WAYS):
            b = [(k >> i) & 1 for i in order]
            grads[piece, b[0], b[1], b[2], b[3]] = full[k * strip : (k + 1) * strip].astype(BF)
        g_copy(piece, 0, order).start()

    def own(piece, depth, order):
        return (piece,) + tuple(bit[b] for b in order[:depth])

    def g_copy(piece, k, order):
        return toward(
            order[k],
            grads.at[own(piece, k, order) + (1 - bit[order[k]],)],
            received[k].at[piece],
            g_send.at[piece, k],
            g_recv.at[piece, k],
        )

    def pass_on(piece, k, order):
        g_copy(piece, k, order).wait_recv()
        here = own(piece, k + 1, order)
        grads[here] = (grads[here].astype(F32) + received[k][piece].astype(F32)).astype(BF)
        g_copy(piece, k + 1, order).start()

    def finish(piece, order):
        g_copy(piece, 3, order).wait_recv()
        return grads[own(piece, 4, order)].astype(F32) + received[3][piece].astype(F32)

    hidden_pieces = hidden // TILE
    down, into, outs, mixes = 0, hidden_pieces, 2 * hidden_pieces, 2 * hidden_pieces + 1
    total = mixes + pairs
    last = hidden_pieces - 1

    dy_load.wait()
    turn(dy)
    vacc[4:5] += jnp.sum(dy[...].astype(F32), axis=0, keepdims=True)
    wo_load.wait()
    win_load.wait()
    wdn_load.wait()
    for part in range(2):
        wo_forward(part)
    for part in range(2):
        wo_copy(1, part).wait_recv()
        wo_copy(3, part).wait_recv()

    per = length // BLOCK

    def middle(n):
        here = rows(n, BLOCK)

        @pl.when(lax.rem(n, per) == 0)
        def _():
            for p in range(pairs):
                o_copy(n // per, p).wait_recv()

        h_buf[here] = dot(o_buf[0, here], wo[0], NT) + dot(o_buf[1, here], wo[1], NT)

        def norm_step(i):
            few = rows(n * (BLOCK // CHUNK) + i, CHUNK)
            resid = h_buf[few] + vin[4:5] + tok[few].astype(F32)
            h_buf[few] = resid
            normed, scale_back = normalize(resid)
            xh2[few] = normed
            r2[few] = scale_back
            c_buf[few] = (normed * vin[1:2] + vin[3:4]).astype(BF)

        loop(BLOCK // CHUNK, norm_step)

        for m in range(hidden // width):

            def hidden_step(i, m=m):
                there = cols(i, 256)
                part = cols(m * wide + i, 256)
                pre = dot(c_buf[here], win[:, part], NN) + vin[6 + m : 7 + m, there]
                back = dot(dy[here], wdn[:, part], NN)
                phi = 0.5 + 0.5 * lax.erf(pre * 0.7071067811865476)
                g_buf[here, part] = (pre * phi).astype(BF)
                slope = phi + pre * (jnp.exp(-0.5 * pre * pre) * 0.3989422804014327)
                low = (back * slope).astype(BF)
                du_buf[here, part] = low
                vacc[1 + m : 2 + m, there] += jnp.sum(low.astype(F32), axis=0, keepdims=True)

            loop(wide, hidden_step)

        def back_step(i):
            there = cols(i, 256)
            grad = dot(du_buf[here], win[rows(i, 256)], NT)
            dc_snd[here, there] = grad.astype(BF)
            dc_copy(n, i).start()
            vacc[6:7, there] += jnp.sum(grad * xh2[here, there], axis=0, keepdims=True)
            vacc[8:9, there] += jnp.sum(grad, axis=0, keepdims=True)

        loop(wide, back_step)

    loop(blocks, middle)

    def mlp_out(s):
        seq = rows(s, length)

        def step(i):
            mlp_snd[seq, cols(i, 256)] = dot(g_buf[seq], wdn[rows(i, 256)], NT).astype(BF)
            mlp_copy(s, i).start()

        loop(wide, step)

    def resid_back(s):
        seq = rows(s, length)
        for n in range(s * per, (s + 1) * per):
            for i in range(wide):
                dc_copy(n, i).wait_recv()

        def step(i):
            here = rows(s * (length // CHUNK) + i, CHUNK)
            grad = dc_snd[here].astype(F32) + dc_rcv[here].astype(F32)
            full = dy[here].astype(F32) + norm_back(grad, xh2[here], r2[here], vin[1:2])
            xh2[here] = full
            dhb[here] = full.astype(BF)
            vacc[3:4] += jnp.sum(full, axis=0, keepdims=True)

        loop(length // CHUNK, step)
        do_buf[seq] = dot(dhb[seq], wo[t], NN).astype(BF)

    def attention_back(s, p):
        seq = rows(s, length)
        mixed = qkv[seq, cols(p, 384)]
        query, keys = mixed[:, :128], stacked(mixed[:, 128:256])
        grad_o = do_buf[seq, cols(p, 128)]
        soft = p_buf[s * pairs + p]
        grad_soft = dot(grad_o, stacked(mixed[:, 256:]), NT)
        parts = []
        for e in range(2):
            one, two = (v[:, e * length : (e + 1) * length] for v in (soft, grad_soft))
            delta = jnp.sum(one * two, axis=-1, keepdims=True)
            parts.append((one * (two - delta)).astype(BF))
        grad_scores = jnp.concatenate(parts, axis=1)
        grad_query = dot(grad_scores, keys, NN) * scale
        grad_keys = dot(grad_scores, query, TN) * scale
        grad_keys = jnp.where(low_half, grad_keys[:length], grad_keys[length:])
        grad_values = dot(soft.astype(BF), grad_o, TN)
        grad_values = jnp.where(low_half, grad_values[:length], grad_values[length:])
        low = [v.astype(BF) for v in (grad_query, grad_keys, grad_values)]
        dp_buf[seq, cols(p, 384)] = jnp.concatenate(low, axis=1)
        vacc[0:1, cols(p, 128)] += jnp.sum(low[0].astype(F32), axis=0, keepdims=True)
        vacc[0:1, cols(pairs + p, 128)] += jnp.sum(low[2].astype(F32), axis=0, keepdims=True)

    def mixed_back(s):
        seq = rows(s, length)

        def step(i):
            here = cols(i, 256)
            grad = dot(dp_buf[seq], wq[rows(i, 256)], NT)
            da_snd[seq, here] = grad.astype(BF)
            vacc[5:6, here] += jnp.sum(grad * xh1[seq, here], axis=0, keepdims=True)
            vacc[7:8, here] += jnp.sum(grad, axis=0, keepdims=True)

        loop(wide, step)

    def send_mixed(s):
        for i in range(wide):
            da_copy(s, i).start()

    def out_copy(n, dst, s):
        here = rows(s, length)
        return pltpu.make_async_copy(out_buf.at[n, here], dst.at[here], out_sem.at[n, s])

    def finish_block(s):
        seq = rows(s, length)

        def step(i):
            mlp_copy(s, i).wait_recv()
            here = seq, cols(i, 256)
            added = mlp_snd[here].astype(F32) + mlp_rcv[here].astype(F32)
            out_buf[0, seq, cols(i, 256)] = (h_buf[here] + (added + vin[5:6, cols(i, 256)])).astype(BF)

        loop(wide, step)
        out_copy(0, block_h, s).start()

    def finish_tokens(s):
        for i in range(wide):
            da_copy(s, i).wait_recv()

        def step(i):
            here = rows(s * (length // CHUNK) + i, CHUNK)
            grad = da_snd[here].astype(F32) + da_rcv[here].astype(F32)
            full = xh2[here] + norm_back(grad, xh1[here], r1[here], vin[0:1])
            out_buf[1, here] = full.astype(BF)

        loop(length // CHUNK, step)
        out_copy(1, gtok_h, s).start()

    def v_copy(k):
        sems = v_send.at[k], v_recv.at[k]
        if k == 0:
            return across(vsum.at[0], vrcv.at[0], *sems)
        return toward(k - 1, vsum.at[k], vrcv.at[k], *sems)

    def v_next(k):
        v_copy(k).wait_recv()
        if k == 0:
            line = lax.broadcasted_iota(jnp.int32, vacc.shape, 0)
            norms = (line >= 5) & (line < 9)
            vsum[1] = jnp.where(norms, vsum[0] + vrcv[0], vsum[0])
        else:
            vsum[k + 1] = vsum[k] + vrcv[k]
        if k < BITS:
            v_copy(k + 1).start()

    order_of = {}
    for piece in range(total):
        first_z = piece in (down + last, into + last, mixes + pairs - 1)
        order_of[piece] = (0, 2, 1, 3) if first_z else (0, 1, 2, 3)

    usual, turned = (0, 1, 2, 3), (0, 2, 1, 3)

    def passes(*what):
        for piece, k in what:
            pass_on(piece, k, order_of[piece])

    def wrap(p, size):
        return p[:, cols(size, TILE)]

    loop(last, lambda i: product(down + i, g_buf[:, cols(i, TILE)], usual))
    product(down + last, g_buf[:, last * TILE :], turned)
    turn(c_buf)

    def into_step(i):
        product(into + i, du_buf[:, cols(i, TILE)], usual)
        pass_on(down + i, 0, usual)

    loop(last, into_step)
    product(into + last, du_buf[:, last * TILE :], turned)
    pass_on(down + last, 0, turned)
    resid_back(0)
    loop(last, lambda i: pass_on(into + i, 0, usual))
    pass_on(into + last, 0, turned)
    loop(pairs, lambda p: attention_back(0, p))
    mixed_back(0)
    send_mixed(0)
    passes((down, 1), (down + 3, 1), (into + 3, 1))
    turn(a_buf)
    passes((down + 1, 1))
    resid_back(1)

    def last_step(p):
        attention_back(1, p)
        product(mixes + p, dp_buf[:, cols(p, 384)], usual)

    loop(pairs - 1, last_step)
    attention_back(1, pairs - 1)
    product(mixes + pairs - 1, dp_buf[:, (pairs - 1) * 384 :], turned)
    mixed_back(1)
    v_copy(0).start()
    send_mixed(1)
    passes((down, 2), (down + 2, 1), (down + 1, 2))
    mlp_out(0)
    passes((down + 3, 2), (into, 1))
    turn(dhb)
    product(outs, o_buf[t], usual)
    mlp_out(1)
    v_next(0)
    passes((mixes + 2, 0))
    v_next(1)
    passes((mixes, 0), (mixes + 1, 0), (outs, 0))
    finish_tokens(0)

    def down_out(i):
        order = turned if i == last else usual
        gdn_ref[:, i * TILE : (i + 1) * TILE] = finish(down + i, order)

    def into_out(i):
        order = turned if i == last else usual
        gin_ref[:, i * TILE : (i + 1) * TILE] = finish(into + i, order)

    def mix_out(p):
        value = finish(mixes + p, order_of[mixes + p])
        for kind in range(3):
            gqkv_ref[kind, :, p * 128 : (p + 1) * 128] = value[:, kind * 128 : (kind + 1) * 128]

    down_out(0)
    passes((down + 2, 2))
    down_out(1)
    passes((into + 1, 1), (into, 2), (into + 3, 2))
    down_out(2)
    down_out(3)
    passes((into + 2, 1), (into + 1, 2), (mixes + 2, 1))
    v_next(2)
    finish_block(0)
    into_out(0)
    passes((mixes, 1), (into + 2, 2))
    into_out(1)
    into_out(3)
    v_next(3)
    passes((mixes + 1, 1), (mixes, 2))
    into_out(2)
    passes((mixes + 2, 2), (outs, 1), (mixes + 1, 2))
    mix_out(0)
    finish_tokens(1)
    passes((outs, 2))
    mix_out(1)
    mix_out(2)
    v_next(4)
    vout[...] = vsum[BITS + 1]
    gout_ref[...] = finish(outs, usual)
    finish_block(1)

    for part in range(2):
        for step in range(4):
            wo_copy(step, part).wait_send()
    for s in range(seqs):
        for p in range(pairs):
            o_copy(s, p).wait_send()
        for i in range(wide):
            da_copy(s, i).wait_send()
            mlp_copy(s, i).wait_send()
        out_copy(0, block_h, s).wait()
        out_copy(1, gtok_h, s).wait()
    for n in range(blocks):
        for i in range(wide):
            dc_copy(n, i).wait_send()

    for piece in range(total):
        for k in range(BITS):
            g_copy(piece, k, order_of[piece]).wait_send()
    for k in range(BITS + 1):
        v_copy(k).wait_send()


def deliver(
    block_h,
    gtok_h,
    gqkv_h,
    gout_h,
    gin_h,
    gdn_h,
    small,
    block_o,
    gtok_o,
    gqkv_o,
    pair_o,
    gout_o,
    ob_o,
    gin_o,
    hb_o,
    gdn_o,
    mb_o,
    gain_o,
    shift_o,
    block_m,
    gtok_m,
    gqkv_m,
    gout_m,
    gin_m,
    gdn_m,
    sem,
):
    big = (
        (block_h, block_m, block_o),
        (gtok_h, gtok_m, gtok_o),
        (gqkv_h, gqkv_m, gqkv_o),
        (gout_h, gout_m, gout_o),
        (gin_h, gin_m, gin_o),
        (gdn_h, gdn_m, gdn_o),
    )
    first = [
        pltpu.make_async_copy(src, mid, sem.at[0, i]) for i, (src, mid, _) in enumerate(big)
    ]
    second = [
        pltpu.make_async_copy(mid, dst, sem.at[1, i]) for i, (_, mid, dst) in enumerate(big)
    ]
    for copy in first:
        copy.start()
    local, width, hidden = pair_o.shape[1], ob_o.shape[0], hb_o.shape[0]
    pair_o[0:1] = small[0:1, :local]
    pair_o[1:2] = small[0:1, local:]
    hb_o[...] = jnp.concatenate([small[1:2], small[2:3]], axis=1).reshape(hidden)
    ob_o[...] = small[3:4].reshape(width)
    mb_o[...] = small[4:5].reshape(width)
    gain_o[...] = small[5:7]
    shift_o[...] = small[7:9]
    for copy, after in zip(first, second):
        copy.wait()
        after.start()
    for copy in second:
        copy.wait()


def body(
    tokens,
    segment_ids,
    w_qkv,
    qv_bias,
    w_out,
    out_bias,
    w_in,
    hidden_bias,
    w_down,
    mlp_bias,
    ln_gain,
    ln_bias,
    cotangent,
    *,
    dp,
):
    seqs, length, width = tokens.shape
    count = seqs * length
    local = w_qkv.shape[2]
    hidden = w_in.shape[1]
    pairs = local // (2 * HEAD)
    stride = dp // WAYS
    strip = width // WAYS
    pieces = 2 * (hidden // TILE) + 1 + pairs
    hbm = pl.BlockSpec(memory_space=pl.ANY)
    vmem = pl.BlockSpec(memory_space=pltpu.VMEM)
    dma = pltpu.SemaphoreType.DMA
    wide = (count, width)
    big = (
        jax.ShapeDtypeStruct(wide, BF),
        jax.ShapeDtypeStruct(wide, BF),
        jax.ShapeDtypeStruct((3, strip, local), F32),
        jax.ShapeDtypeStruct((strip, local), F32),
        jax.ShapeDtypeStruct((strip, hidden), F32),
        jax.ShapeDtypeStruct((strip, hidden), F32),
    )
    outs = pl.pallas_call(
        functools.partial(kernel, stride),
        out_shape=big + (jax.ShapeDtypeStruct((16, width), F32),),
        in_specs=[hbm, vmem, hbm, vmem, hbm, vmem, hbm, vmem, hbm, vmem, vmem, vmem, hbm],
        out_specs=(hbm, hbm, vmem, vmem, vmem, vmem, vmem),
        scratch_shapes=[
            pltpu.VMEM(wide, BF),
            pltpu.VMEM(wide, BF),
            pltpu.VMEM((width, 3 * local), BF),
            pltpu.VMEM((2, width, local), BF),
            pltpu.VMEM((width, hidden), BF),
            pltpu.VMEM((width, hidden), BF),
            pltpu.VMEM((16, width), F32),
            pltpu.VMEM(wide, BF),
            pltpu.VMEM(wide, F32),
            pltpu.VMEM((count, 1), F32),
            pltpu.VMEM((count, 3 * local), BF),
            pltpu.VMEM((seqs * pairs, length, 2 * length), F32),
            pltpu.VMEM((2, count, local), BF),
            pltpu.VMEM(wide, F32),
            pltpu.VMEM(wide, F32),
            pltpu.VMEM((count, 1), F32),
            pltpu.VMEM(wide, BF),
            pltpu.VMEM((count, hidden), BF),
            pltpu.VMEM((count, hidden), BF),
            pltpu.VMEM(wide, BF),
            pltpu.VMEM(wide, BF),
            pltpu.VMEM(wide, BF),
            pltpu.VMEM(wide, BF),
            pltpu.VMEM(wide, BF),
            pltpu.VMEM(wide, BF),
            pltpu.VMEM((count, local), BF),
            pltpu.VMEM(wide, BF),
            pltpu.VMEM((count, 3 * local), BF),
            pltpu.VMEM((2, count, width), BF),
            pltpu.VMEM((width, count), BF),
            pltpu.VMEM((pieces, 2, 2, 2, 2, strip, TILE), BF),
            pltpu.VMEM((pieces, 2, 2, 2, strip, TILE), BF),
            pltpu.VMEM((pieces, 2, 2, strip, TILE), BF),
            pltpu.VMEM((pieces, 2, strip, TILE), BF),
            pltpu.VMEM((pieces, strip, TILE), BF),
            pltpu.VMEM((BITS + 2, 16, width), F32),
            pltpu.VMEM((BITS + 1, 16, width), F32),
            dma((5 + 3 * pairs,)),
            dma((4, 2)),
            dma((4, 2)),
            dma((seqs, pairs)),
            dma((seqs, pairs)),
            dma((3, count // BLOCK, width // 256)),
            dma((3, count // BLOCK, width // 256)),
            dma((pieces, BITS)),
            dma((pieces, BITS)),
            dma((BITS + 1,)),
            dma((BITS + 1,)),
            dma((2, seqs)),
        ],
        compiler_params=pltpu.CompilerParams(
            collective_id=0, has_side_effects=True, vmem_limit_bytes=60 * 2**20
        ),
        cost_estimate=pl.CostEstimate(
            flops=12 * 10**9, bytes_accessed=12 * 10**6, transcendentals=4 * 10**6
        ),
    )(
        tokens.reshape(wide),
        segment_ids,
        w_qkv.transpose(1, 0, 2),
        qv_bias,
        w_out,
        out_bias,
        w_in,
        hidden_bias,
        w_down,
        mlp_bias,
        ln_gain,
        ln_bias,
        cotangent.reshape(wide),
    )
    if stride > 1:
        groups = [[g * stride + i for i in range(stride)] for g in range(WAYS)]
        scatter = functools.partial(
            lax.psum_scatter, axis_name="dp", axis_index_groups=groups, tiled=True
        )
        outs = (
            *outs[:2],
            scatter(outs[2], scatter_dimension=1),
            *[scatter(v, scatter_dimension=0) for v in outs[3:6]],
            lax.psum(outs[6], "dp", axis_index_groups=groups),
        )
    shapes = [
        outs[0],
        outs[1],
        outs[2],
        jax.ShapeDtypeStruct((2, local), F32),
        outs[3],
        jax.ShapeDtypeStruct((width,), F32),
        outs[4],
        jax.ShapeDtypeStruct((hidden,), F32),
        outs[5],
        jax.ShapeDtypeStruct((width,), F32),
        jax.ShapeDtypeStruct((2, width), F32),
        jax.ShapeDtypeStruct((2, width), F32),
    ]
    placed = [hbm, hbm, hbm, vmem, hbm, vmem, hbm, vmem, hbm, vmem, vmem, vmem]
    done = pl.pallas_call(
        deliver,
        out_shape=tuple(jax.ShapeDtypeStruct(v.shape, v.dtype) for v in shapes),
        in_specs=[hbm] * 6 + [vmem],
        out_specs=tuple(placed),
        scratch_shapes=[pltpu.VMEM(v.shape, v.dtype) for v in outs[:6]] + [dma((2, 6))],
    )(*outs)
    return (
        done[0].reshape(tokens.shape),
        done[1].reshape(tokens.shape),
        done[2].transpose(1, 0, 2),
        *done[3:],
    )


def solution(mesh):
    return jax.shard_map(
        functools.partial(body, dp=mesh.shape["dp"]),
        mesh=mesh,
        in_specs=(
            P("dp", None, None),
            P("dp", None),
            P(None, None, "tensor"),
            P(None, "tensor"),
            P(None, "tensor"),
            P(),
            P(None, "tensor"),
            P("tensor"),
            P(None, "tensor"),
            P(),
            P(),
            P(),
            P("dp", None, None),
        ),
        out_specs=(
            P("dp", None, None),
            P("dp", None, None),
            P("dp", None, "tensor"),
            P(None, "tensor"),
            P("dp", "tensor"),
            P(),
            P("dp", "tensor"),
            P("tensor"),
            P("dp", "tensor"),
            P(),
            P(),
            P(),
        ),
        check_vma=False,
    )
```

time: 103 us -> 90.4 us (0.88)
  local copies, waits for them, and re-layouts: 15.1 us -> 0 us
  Pallas kernels: 86.5 us -> 89.5 us
    unnamed x15 -> x0, local copies, waits for them, and re-layouts: 6.89 us -> none
    pallas_call x1 -> x2, Pallas kernels: 86.5 us -> 89.5 us  [the longest x1 85.4 us: body(): pl.pallas_call(functools.partial(kernel, stride), out_shape=big + (jax.Sh...]
    slice x2 -> x0, local copies, waits for them, and re-layouts: 2.97 us -> none  [the longest x1 1.5 us: body(): small[7:9]]
    concatenate x1 -> x0, local copies, waits for them, and re-layouts: 1.95 us -> none  [body(): jnp.concatenate([ln_gain.astype(F32), ln_bias.astype(F32), out_bias.astyp...]
    broadcast_in_dim x3 -> x0, local copies, waits for them, and re-layouts: 1.37 us -> none  [the longest x1 0.68 us: body(): out_bias.astype(F32)[None]]
    reshape x2 -> x0, local copies, waits for them, and re-layouts: 1.31 us -> none  [the longest x1 0.7 us: body(): hidden_bias.astype(F32).reshape(2, width)]
where the time goes in v2:
time: 90.4 us; the launch traced here: 90.2 us
  Pallas kernels  89.5 us (99%)
    pallas_call x1, Pallas kernels, body(): pl.pallas_call(functools.partial(kernel, stride), out_shape=big + (jax.Sh...  85.4 us
    pallas_call x1, Pallas kernels, body(): pl.pallas_call(deliver, out_shape=tuple((jax.ShapeDtypeStruct(v.shape, v....  4.08 us

profile of v2, /device:TPU:0, one launch (start us, length us, event | category | flops | bytes accessed | tf_op | source)
XLA Modules:
  0.0 90.2 jit_solution(7257698354615237792)
XLA Ops:
  0.6 85.4 %shard_map.220 = (bf16[512,768]{1,0:T(8,128)(2,1)}, bf16[512,768]{1,0:T(8,128)(2,1)}, f32[3,48,384]{2,1,0:T(8,128)}, f32[48,384]{1,0:T(8,128)}, f32[48,1536]{1,0...) custom-call(bf16[512,768]{1,0:T(8,128)(2,1)} %bitcast.7, s32[2,256]{1,0:T(2,128)} %seg_ref.1, ...), custom_call_target="tpu_custom_call" | custom-call | flops 12000000000 | bytes 12000000 | tf_op jit(solution)/shard_map/pallas_call | solution.py:754
  86.1 4.1 %shard_map.221 = (bf16[512,768]{1,0:T(8,128)(2,1)}, bf16[512,768]{1,0:T(8,128)(2,1)}, f32[3,48,384]{2,1,0:T(8,128)}, f32[2,384]{1,0:T(2,128)}, f32[48,384]{1,0:T...) custom-call(bf16[512,768]{1,0:T(8,128)(2,1)} %get-tuple-element.31.b, ...), custom_call_target="tpu_custom_call" | custom-call | tf_op jit(solution)/shard_map/pallas_call | solution.py:857

commit v3 on v2

--- a/solution.py
+++ b/solution.py
@@ -19,6 +19,36 @@
 CHUNK = 64
 TILE = 384
 
+PLAN = (
+    ("prod", 6), ("prod", 1), ("prod", 7), ("pass", 6, 0), ("pass", 1, 0), ("prod", 2), ("prod", 3),
+    ("prod", 4), ("pass", 3, 0), ("pass", 7, 0), ("pass", 2, 0), ("prod", 0), ("resid", 0),
+    ("pass", 1, 1), ("pass", 0, 0), ("attb", 0, 2), ("pass", 4, 0), ("attb", 0, 0), ("pass", 6, 1),
+    ("mlp", 0), ("prod", 5), ("pass", 5, 0), ("attb", 0, 1), ("resid", 1), ("attb", 1, 1),
+    ("pass", 4, 1), ("pass", 7, 1), ("mixb", 0), ("pass", 1, 2), ("prod", 10), ("attb", 1, 0),
+    ("prod", 9), ("pass", 2, 1), ("sda", 0), ("pass", 10, 0), ("pass", 9, 0), ("pass", 6, 2),
+    ("attb", 1, 2), ("pass", 0, 1), ("mixb", 1), ("prod", 8), ("v", 0), ("pass", 4, 2),
+    ("pass", 8, 0), ("pass", 7, 2), ("pass", 3, 1), ("pass", 2, 2), ("fin", 1), ("prod", 11),
+    ("pass", 9, 1), ("pass", 10, 1), ("sda", 1), ("pass", 0, 2), ("pass", 11, 0), ("pass", 5, 1),
+    ("pass", 3, 2), ("ft", 0), ("v", 1), ("pass", 8, 1), ("pass", 10, 2), ("fin", 2), ("fb", 0),
+    ("pass", 5, 2), ("pass", 9, 2), ("v", 2), ("fin", 6), ("fin", 7), ("mlp", 1), ("pass", 11, 1),
+    ("fin", 4), ("pass", 8, 2), ("v", 3), ("pass", 11, 2), ("fin", 3), ("v", 4), ("fin", 5),
+    ("ft", 1), ("fin", 9), ("fin", 11), ("fin", 0), ("fin", 8), ("v", 5), ("fin", 10), ("fb", 1),
+)
+HALVINGS = (
+    (0, 2, 1, 3),
+    (0, 1, 2, 3),
+    (0, 1, 2, 3),
+    (0, 2, 1, 3),
+    (0, 1, 2, 3),
+    (0, 1, 2, 3),
+    (0, 2, 1, 3),
+    (0, 2, 1, 3),
+    (0, 1, 2, 3),
+    (0, 2, 1, 3),
+    (0, 1, 2, 3),
+    (0, 1, 2, 3),
+)
+
 NN = ((1,), (0,))
 NT = ((1,), (1,))
 TN = ((0,), (0,))
@@ -36,12 +66,18 @@
     lax.fori_loop(0, count, run, 0)
 
 
-def cols(i, width):
-    return pl.ds(pl.multiple_of(i * width, width), width)
-
-
-def rows(i, height):
-    return pl.ds(pl.multiple_of(i * height, height), height)
+def each(count, step):
+    for i in range(count):
+        step(i)
+
+
+def rows(i, size):
+    if isinstance(i, int):
+        return slice(i * size, (i + 1) * size)
+    return pl.ds(pl.multiple_of(i * size, size), size)
+
+
+cols = rows
 
 
 def kernel(
@@ -59,8 +95,8 @@
     gain_ref,
     shift_ref,
     dy_h,
-    block_h,
-    gtok_h,
+    block_ref,
+    gtok_ref,
     gqkv_ref,
     gout_ref,
     gin_ref,
@@ -94,8 +130,6 @@
     do_buf,
     dhb,
     dp_buf,
-    out_buf,
-    l_t,
     grads,
     r0_buf,
     r1_buf,
@@ -114,7 +148,6 @@
     g_recv,
     v_send,
     v_recv,
-    out_sem,
 ):
     d = lax.axis_index("dp")
     t = lax.axis_index("tensor")
@@ -275,7 +308,7 @@
             r1[here] = scale_back
             a_buf[here] = (normed * vin[0:1] + vin[2:3]).astype(BF)
 
-        loop(length // CHUNK, step)
+        each(length // CHUNK, step)
 
     def attention(s):
         seq = rows(s, length)
@@ -305,10 +338,11 @@
             ).astype(BF)
             o_copy(s, p).start()
 
-        loop(pairs, pair_step)
+        each(pairs, pair_step)
 
     tok_load.wait()
     norm_one(0)
+    norm_one(1)
     pl.semaphore_wait(barrier, BITS + 1)
     wo_copy(0, 0).start()
     wo_copy(0, 1).start()
@@ -316,19 +350,14 @@
         copy.wait()
     attention(0)
     wo_share(0)
-    norm_one(1)
     wo_share(1)
     attention(1)
 
-    def turn(src):
-        for s in range(seqs):
-            l_t[:, s * length : (s + 1) * length] = src[s * length : (s + 1) * length].T
-
     strip = width // WAYS
     received = [r0_buf, r1_buf, r2_buf, r3_buf]
 
-    def product(piece, right, order):
-        full = dot(l_t[...], right, NN)
+    def product(piece, left, right, order):
+        full = dot(left[...], right, TN)
         for k in range(WAYS):
             b = [(k >> i) & 1 for i in order]
             grads[piece, b[0], b[1], b[2], b[3]] = full[k * strip : (k + 1) * strip].astype(BF)
@@ -359,10 +388,8 @@
     hidden_pieces = hidden // TILE
     down, into, outs, mixes = 0, hidden_pieces, 2 * hidden_pieces, 2 * hidden_pieces + 1
     total = mixes + pairs
-    last = hidden_pieces - 1
 
     dy_load.wait()
-    turn(dy)
     vacc[4:5] += jnp.sum(dy[...].astype(F32), axis=0, keepdims=True)
     wo_load.wait()
     win_load.wait()
@@ -394,7 +421,7 @@
             r2[few] = scale_back
             c_buf[few] = (normed * vin[1:2] + vin[3:4]).astype(BF)
 
-        loop(BLOCK // CHUNK, norm_step)
+        each(BLOCK // CHUNK, norm_step)
 
         for m in range(hidden // width):
 
@@ -410,7 +437,7 @@
                 du_buf[here, part] = low
                 vacc[1 + m : 2 + m, there] += jnp.sum(low.astype(F32), axis=0, keepdims=True)
 
-            loop(wide, hidden_step)
+            each(wide, hidden_step)
 
         def back_step(i):
             there = cols(i, 256)
@@ -420,7 +447,7 @@
             vacc[6:7, there] += jnp.sum(grad * xh2[here, there], axis=0, keepdims=True)
             vacc[8:9, there] += jnp.sum(grad, axis=0, keepdims=True)
 
-        loop(wide, back_step)
+        each(wide, back_step)
 
     loop(blocks, middle)
 
@@ -431,7 +458,7 @@
             mlp_snd[seq, cols(i, 256)] = dot(g_buf[seq], wdn[rows(i, 256)], NT).astype(BF)
             mlp_copy(s, i).start()
 
-        loop(wide, step)
+        each(wide, step)
 
     def resid_back(s):
         seq = rows(s, length)
@@ -447,7 +474,7 @@
             dhb[here] = full.astype(BF)
             vacc[3:4] += jnp.sum(full, axis=0, keepdims=True)
 
-        loop(length // CHUNK, step)
+        each(length // CHUNK, step)
         do_buf[seq] = dot(dhb[seq], wo[t], NN).astype(BF)
 
     def attention_back(s, p):
@@ -483,15 +510,11 @@
             vacc[5:6, here] += jnp.sum(grad * xh1[seq, here], axis=0, keepdims=True)
             vacc[7:8, here] += jnp.sum(grad, axis=0, keepdims=True)
 
-        loop(wide, step)
+        each(wide, step)
 
     def send_mixed(s):
         for i in range(wide):
             da_copy(s, i).start()
-
-    def out_copy(n, dst, s):
-        here = rows(s, length)
-        return pltpu.make_async_copy(out_buf.at[n, here], dst.at[here], out_sem.at[n, s])
 
     def finish_block(s):
         seq = rows(s, length)
@@ -500,10 +523,9 @@
             mlp_copy(s, i).wait_recv()
             here = seq, cols(i, 256)
             added = mlp_snd[here].astype(F32) + mlp_rcv[here].astype(F32)
-            out_buf[0, seq, cols(i, 256)] = (h_buf[here] + (added + vin[5:6, cols(i, 256)])).astype(BF)
-
-        loop(wide, step)
-        out_copy(0, block_h, s).start()
+            block_ref[seq, cols(i, 256)] = (h_buf[here] + (added + vin[5:6, cols(i, 256)])).astype(BF)
+
+        each(wide, step)
 
     def finish_tokens(s):
         for i in range(wide):
@@ -513,10 +535,9 @@
             here = rows(s * (length // CHUNK) + i, CHUNK)
             grad = da_snd[here].astype(F32) + da_rcv[here].astype(F32)
             full = xh2[here] + norm_back(grad, xh1[here], r1[here], vin[0:1])
-            out_buf[1, here] = full.astype(BF)
-
-        loop(length // CHUNK, step)
-        out_copy(1, gtok_h, s).start()
+            gtok_ref[here] = full.astype(BF)
+
+        each(length // CHUNK, step)
 
     def v_copy(k):
         sems = v_send.at[k], v_recv.at[k]
@@ -535,103 +556,52 @@
         if k < BITS:
             v_copy(k + 1).start()
 
-    order_of = {}
-    for piece in range(total):
-        first_z = piece in (down + last, into + last, mixes + pairs - 1)
-        order_of[piece] = (0, 2, 1, 3) if first_z else (0, 1, 2, 3)
-
-    usual, turned = (0, 1, 2, 3), (0, 2, 1, 3)
-
-    def passes(*what):
-        for piece, k in what:
-            pass_on(piece, k, order_of[piece])
-
-    def wrap(p, size):
-        return p[:, cols(size, TILE)]
-
-    loop(last, lambda i: product(down + i, g_buf[:, cols(i, TILE)], usual))
-    product(down + last, g_buf[:, last * TILE :], turned)
-    turn(c_buf)
-
-    def into_step(i):
-        product(into + i, du_buf[:, cols(i, TILE)], usual)
-        pass_on(down + i, 0, usual)
-
-    loop(last, into_step)
-    product(into + last, du_buf[:, last * TILE :], turned)
-    pass_on(down + last, 0, turned)
-    resid_back(0)
-    loop(last, lambda i: pass_on(into + i, 0, usual))
-    pass_on(into + last, 0, turned)
-    loop(pairs, lambda p: attention_back(0, p))
-    mixed_back(0)
-    send_mixed(0)
-    passes((down, 1), (down + 3, 1), (into + 3, 1))
-    turn(a_buf)
-    passes((down + 1, 1))
-    resid_back(1)
-
-    def last_step(p):
-        attention_back(1, p)
-        product(mixes + p, dp_buf[:, cols(p, 384)], usual)
-
-    loop(pairs - 1, last_step)
-    attention_back(1, pairs - 1)
-    product(mixes + pairs - 1, dp_buf[:, (pairs - 1) * 384 :], turned)
-    mixed_back(1)
-    v_copy(0).start()
-    send_mixed(1)
-    passes((down, 2), (down + 2, 1), (down + 1, 2))
-    mlp_out(0)
-    passes((down + 3, 2), (into, 1))
-    turn(dhb)
-    product(outs, o_buf[t], usual)
-    mlp_out(1)
-    v_next(0)
-    passes((mixes + 2, 0))
-    v_next(1)
-    passes((mixes, 0), (mixes + 1, 0), (outs, 0))
-    finish_tokens(0)
-
-    def down_out(i):
-        order = turned if i == last else usual
-        gdn_ref[:, i * TILE : (i + 1) * TILE] = finish(down + i, order)
-
-    def into_out(i):
-        order = turned if i == last else usual
-        gin_ref[:, i * TILE : (i + 1) * TILE] = finish(into + i, order)
-
-    def mix_out(p):
-        value = finish(mixes + p, order_of[mixes + p])
-        for kind in range(3):
-            gqkv_ref[kind, :, p * 128 : (p + 1) * 128] = value[:, kind * 128 : (kind + 1) * 128]
-
-    down_out(0)
-    passes((down + 2, 2))
-    down_out(1)
-    passes((into + 1, 1), (into, 2), (into + 3, 2))
-    down_out(2)
-    down_out(3)
-    passes((into + 2, 1), (into + 1, 2), (mixes + 2, 1))
-    v_next(2)
-    finish_block(0)
-    into_out(0)
-    passes((mixes, 1), (into + 2, 2))
-    into_out(1)
-    into_out(3)
-    v_next(3)
-    passes((mixes + 1, 1), (mixes, 2))
-    into_out(2)
-    passes((mixes + 2, 2), (outs, 1), (mixes + 1, 2))
-    mix_out(0)
-    finish_tokens(1)
-    passes((outs, 2))
-    mix_out(1)
-    mix_out(2)
-    v_next(4)
-    vout[...] = vsum[BITS + 1]
-    gout_ref[...] = finish(outs, usual)
-    finish_block(1)
+    def prod(piece):
+        order = HALVINGS[piece]
+        if piece < into:
+            product(piece, dy, g_buf[:, cols(piece, TILE)], order)
+        elif piece < outs:
+            product(piece, c_buf, du_buf[:, cols(piece - into, TILE)], order)
+        elif piece < mixes:
+            product(piece, dhb, o_buf[t], order)
+        else:
+            product(piece, a_buf, dp_buf[:, cols(piece - mixes, 384)], order)
+
+    def fin(piece):
+        value = finish(piece, HALVINGS[piece])
+        if piece < into:
+            gdn_ref[:, cols(piece, TILE)] = value
+        elif piece < outs:
+            gin_ref[:, cols(piece - into, TILE)] = value
+        elif piece < mixes:
+            gout_ref[...] = value
+        else:
+            for kind in range(3):
+                gqkv_ref[kind, :, cols(piece - mixes, 128)] = value[:, cols(kind, 128)]
+
+    def small(k):
+        if k == 0:
+            v_copy(0).start()
+        else:
+            v_next(k - 1)
+        if k == BITS + 1:
+            vout[...] = vsum[k]
+
+    steps = {
+        "prod": prod,
+        "pass": lambda piece, k: pass_on(piece, k, HALVINGS[piece]),
+        "fin": fin,
+        "resid": resid_back,
+        "attb": attention_back,
+        "mixb": mixed_back,
+        "sda": send_mixed,
+        "mlp": mlp_out,
+        "fb": finish_block,
+        "ft": finish_tokens,
+        "v": small,
+    }
+    for name, *which in PLAN:
+        steps[name](*which)
 
     for part in range(2):
         for step in range(4):
@@ -642,26 +612,24 @@
         for i in range(wide):
             da_copy(s, i).wait_send()
             mlp_copy(s, i).wait_send()
-        out_copy(0, block_h, s).wait()
-        out_copy(1, gtok_h, s).wait()
     for n in range(blocks):
         for i in range(wide):
             dc_copy(n, i).wait_send()
 
     for piece in range(total):
         for k in range(BITS):
-            g_copy(piece, k, order_of[piece]).wait_send()
+            g_copy(piece, k, HALVINGS[piece]).wait_send()
     for k in range(BITS + 1):
         v_copy(k).wait_send()
 
 
 def deliver(
-    block_h,
-    gtok_h,
-    gqkv_h,
-    gout_h,
-    gin_h,
-    gdn_h,
+    block_v,
+    gtok_v,
+    gqkv_v,
+    gout_v,
+    gin_v,
+    gdn_v,
     small,
     block_o,
     gtok_o,
@@ -675,29 +643,18 @@
     mb_o,
     gain_o,
     shift_o,
-    block_m,
-    gtok_m,
-    gqkv_m,
-    gout_m,
-    gin_m,
-    gdn_m,
     sem,
 ):
     big = (
-        (block_h, block_m, block_o),
-        (gtok_h, gtok_m, gtok_o),
-        (gqkv_h, gqkv_m, gqkv_o),
-        (gout_h, gout_m, gout_o),
-        (gin_h, gin_m, gin_o),
-        (gdn_h, gdn_m, gdn_o),
+        (block_v, block_o),
+        (gtok_v, gtok_o),
+        (gqkv_v, gqkv_o),
+        (gout_v, gout_o),
+        (gin_v, gin_o),
+        (gdn_v, gdn_o),
     )
-    first = [
-        pltpu.make_async_copy(src, mid, sem.at[0, i]) for i, (src, mid, _) in enumerate(big)
-    ]
-    second = [
-        pltpu.make_async_copy(mid, dst, sem.at[1, i]) for i, (_, mid, dst) in enumerate(big)
-    ]
-    for copy in first:
+    copies = [pltpu.make_async_copy(src, dst, sem.at[i]) for i, (src, dst) in enumerate(big)]
+    for copy in copies:
         copy.start()
     local, width, hidden = pair_o.shape[1], ob_o.shape[0], hb_o.shape[0]
     pair_o[0:1] = small[0:1, :local]
@@ -707,10 +664,7 @@
     mb_o[...] = small[4:5].reshape(width)
     gain_o[...] = small[5:7]
     shift_o[...] = small[7:9]
-    for copy, after in zip(first, second):
-        copy.wait()
-        after.start()
-    for copy in second:
+    for copy in copies:
         copy.wait()
 
 
@@ -744,18 +698,18 @@
     dma = pltpu.SemaphoreType.DMA
     wide = (count, width)
     big = (
-        jax.ShapeDtypeStruct(wide, BF),
-        jax.ShapeDtypeStruct(wide, BF),
-        jax.ShapeDtypeStruct((3, strip, local), F32),
-        jax.ShapeDtypeStruct((strip, local), F32),
-        jax.ShapeDtypeStruct((strip, hidden), F32),
-        jax.ShapeDtypeStruct((strip, hidden), F32),
+        pltpu.VMEM(wide, BF),
+        pltpu.VMEM(wide, BF),
+        pltpu.VMEM((3, strip, local), F32),
+        pltpu.VMEM((strip, local), F32),
+        pltpu.VMEM((strip, hidden), F32),
+        pltpu.VMEM((strip, hidden), F32),
     )
     outs = pl.pallas_call(
         functools.partial(kernel, stride),
-        out_shape=big + (jax.ShapeDtypeStruct((16, width), F32),),
+        out_shape=big + (pltpu.VMEM((16, width), F32),),
         in_specs=[hbm, vmem, hbm, vmem, hbm, vmem, hbm, vmem, hbm, vmem, vmem, vmem, hbm],
-        out_specs=(hbm, hbm, vmem, vmem, vmem, vmem, vmem),
+        out_specs=(vmem,) * 7,
         scratch_shapes=[
             pltpu.VMEM(wide, BF),
             pltpu.VMEM(wide, BF),
@@ -785,8 +739,6 @@
             pltpu.VMEM((count, local), BF),
             pltpu.VMEM(wide, BF),
             pltpu.VMEM((count, 3 * local), BF),
-            pltpu.VMEM((2, count, width), BF),
-            pltpu.VMEM((width, count), BF),
             pltpu.VMEM((pieces, 2, 2, 2, 2, strip, TILE), BF),
             pltpu.VMEM((pieces, 2, 2, 2, strip, TILE), BF),
             pltpu.VMEM((pieces, 2, 2, strip, TILE), BF),
@@ -805,10 +757,9 @@
             dma((pieces, BITS)),
             dma((BITS + 1,)),
             dma((BITS + 1,)),
-            dma((2, seqs)),
         ],
         compiler_params=pltpu.CompilerParams(
-            collective_id=0, has_side_effects=True, vmem_limit_bytes=60 * 2**20
+            collective_id=0, has_side_effects=True, vmem_limit_bytes=56 * 2**20
         ),
         cost_estimate=pl.CostEstimate(
             flops=12 * 10**9, bytes_accessed=12 * 10**6, transcendentals=4 * 10**6
@@ -857,10 +808,10 @@
     done = pl.pallas_call(
         deliver,
         out_shape=tuple(jax.ShapeDtypeStruct(v.shape, v.dtype) for v in shapes),
-        in_specs=[hbm] * 6 + [vmem],
+        in_specs=[vmem] * 7,
         out_specs=tuple(placed),
-        scratch_shapes=[pltpu.VMEM(v.shape, v.dtype) for v in outs[:6]] + [dma((2, 6))],
-    )(*outs)
+        scratch_shapes=[dma((6,))],
+    )(*[pltpu.with_memory_space_constraint(v, pltpu.VMEM) for v in outs])
     return (
         done[0].reshape(tokens.shape),
         done[1].reshape(tokens.shape),

time: 90.4 us -> 76.5 us (0.85)
  Pallas kernels: 89.5 us -> 75.5 us
    pallas_call x1, Pallas kernels: 85.4 us -> 73.4 us  [body(): pl.pallas_call(functools.partial(kernel, stride), out_shape=big + (pltpu....]
    pallas_call x1, Pallas kernels: 4.08 us -> 2.1 us  [body(): pl.pallas_call(deliver, out_shape=tuple((jax.ShapeDtypeStruct(v.shape, v....]
where the time goes in v3:
time: 76.5 us; the launch traced here: 76.3 us
  Pallas kernels  75.5 us (99%)
  between operations  0.84 us (1%)
    pallas_call x1, Pallas kernels, body(): pl.pallas_call(functools.partial(kernel, stride), out_shape=big + (pltpu....  73.4 us
    pallas_call x1, Pallas kernels, body(): pl.pallas_call(deliver, out_shape=tuple((jax.ShapeDtypeStruct(v.shape, v....  2.1 us

profile of v3, /device:TPU:0, one launch (start us, length us, event | category | flops | bytes accessed | tf_op | source)
XLA Modules:
  0.0 76.3 jit_solution(5706548204521156415)
XLA Ops:
  0.6 73.4 %shard_map.220 = (bf16[512,768]{1,0:T(8,128)(2,1)S(1)}, bf16[512,768]{1,0:T(8,128)(2,1)S(1)}, f32[3,48,384]{2,1,0:T(8,128)S(1)}, f32[48,384]{1,0:T(8,128)S(1)}, ...) custom-call(bf16[512,768]{1,0:T(8,128)(2,1)} %bitcast.7, s32[2,256]{1,0:T(2,128)} %seg_ref.1, ...), custom_call_target="tpu_custom_call" | custom-call | flops 12000000000 | bytes 12000000 | tf_op jit(solution)/shard_map/pallas_call | solution.py:708
  74.0 2.1 %shard_map.221 = (bf16[512,768]{1,0:T(8,128)(2,1)}, bf16[512,768]{1,0:T(8,128)(2,1)}, f32[3,48,384]{2,1,0:T(8,128)}, f32[2,384]{1,0:T(2,128)}, f32[48,384]{1,0:T...) custom-call(bf16[512,768]{1,0:T(8,128)(2,1)S(1)} %get-tuple-element., ...), custom_call_target="tpu_custom_call" | custom-call | tf_op jit(solution)/shard_map/pallas_call | solution.py:808

commit v4 on v3

--- a/solution.py
+++ b/solution.py
@@ -20,22 +20,25 @@
 TILE = 384
 
 PLAN = (
-    ("prod", 6), ("prod", 1), ("prod", 7), ("pass", 6, 0), ("pass", 1, 0), ("prod", 2), ("prod", 3),
-    ("prod", 4), ("pass", 3, 0), ("pass", 7, 0), ("pass", 2, 0), ("prod", 0), ("resid", 0),
-    ("pass", 1, 1), ("pass", 0, 0), ("attb", 0, 2), ("pass", 4, 0), ("attb", 0, 0), ("pass", 6, 1),
-    ("mlp", 0), ("prod", 5), ("pass", 5, 0), ("attb", 0, 1), ("resid", 1), ("attb", 1, 1),
-    ("pass", 4, 1), ("pass", 7, 1), ("mixb", 0), ("pass", 1, 2), ("prod", 10), ("attb", 1, 0),
-    ("prod", 9), ("pass", 2, 1), ("sda", 0), ("pass", 10, 0), ("pass", 9, 0), ("pass", 6, 2),
-    ("attb", 1, 2), ("pass", 0, 1), ("mixb", 1), ("prod", 8), ("v", 0), ("pass", 4, 2),
-    ("pass", 8, 0), ("pass", 7, 2), ("pass", 3, 1), ("pass", 2, 2), ("fin", 1), ("prod", 11),
-    ("pass", 9, 1), ("pass", 10, 1), ("sda", 1), ("pass", 0, 2), ("pass", 11, 0), ("pass", 5, 1),
-    ("pass", 3, 2), ("ft", 0), ("v", 1), ("pass", 8, 1), ("pass", 10, 2), ("fin", 2), ("fb", 0),
-    ("pass", 5, 2), ("pass", 9, 2), ("v", 2), ("fin", 6), ("fin", 7), ("mlp", 1), ("pass", 11, 1),
-    ("fin", 4), ("pass", 8, 2), ("v", 3), ("pass", 11, 2), ("fin", 3), ("v", 4), ("fin", 5),
-    ("ft", 1), ("fin", 9), ("fin", 11), ("fin", 0), ("fin", 8), ("v", 5), ("fin", 10), ("fb", 1),
+    ("prod", 0), ("prod", 7), ("mb", 1), ("pass", 0, 0), ("prod", 4), ("pass", 7, 0), ("prod", 2),
+    ("prod", 1), ("prod", 3), ("resid", 0), ("pass", 2, 0), ("pass", 3, 0), ("pass", 4, 0),
+    ("pass", 1, 0), ("resid", 1), ("prod", 8), ("pass", 0, 1), ("prod", 12), ("pass", 8, 0),
+    ("attb", 0, 1), ("mlp", 1), ("pass", 7, 1), ("attb", 1, 0), ("prod", 5), ("pass", 2, 1),
+    ("pass", 3, 1), ("attb", 0, 0), ("attb", 0, 2), ("pass", 5, 0), ("attb", 1, 2), ("prod", 11),
+    ("mixb", 0), ("pass", 1, 1), ("pass", 12, 0), ("pass", 0, 2), ("attb", 1, 1), ("mixb", 1),
+    ("prod", 6), ("v", 0), ("pass", 2, 2), ("sda", 0), ("pass", 8, 1), ("pass", 3, 2),
+    ("pass", 11, 0), ("prod", 9), ("prod", 10), ("pass", 5, 1), ("mlp", 0), ("pass", 6, 0),
+    ("fb", 1), ("v", 1), ("v", 2), ("pass", 1, 2), ("pass", 12, 1), ("pass", 11, 1), ("sda", 1),
+    ("pass", 8, 2), ("pass", 5, 2), ("pass", 9, 0), ("pass", 7, 2), ("v", 3), ("pass", 12, 2),
+    ("pass", 10, 0), ("pass", 6, 1), ("pass", 11, 2), ("v", 4), ("ft", 0), ("fin", 3),
+    ("pass", 4, 1), ("pass", 9, 1), ("pass", 6, 2), ("fo",), ("pass", 10, 1), ("fin", 0), ("ft", 1),
+    ("pass", 4, 2), ("pass", 9, 2), ("fin", 5), ("fin", 1), ("pass", 10, 2), ("fb", 0), ("fin", 7),
+    ("fin", 4), ("fin", 2), ("fin", 9), ("fin", 6), ("v", 5), ("foe",), ("fin", 11), ("fin", 10),
+    ("gt", 0), ("gt", 1),
 )
 HALVINGS = (
-    (0, 2, 1, 3),
+    (0, 1, 2, 3),
+    (0, 1, 2, 3),
     (0, 1, 2, 3),
     (0, 1, 2, 3),
     (0, 2, 1, 3),
@@ -44,8 +47,8 @@
     (0, 2, 1, 3),
     (0, 2, 1, 3),
     (0, 1, 2, 3),
+    (0, 1, 2, 3),
     (0, 2, 1, 3),
-    (0, 1, 2, 3),
     (0, 1, 2, 3),
 )
 
@@ -56,14 +59,6 @@
 
 def dot(a, b, dims):
     return lax.dot_general(a, b, (dims, ((), ())), preferred_element_type=F32)
-
-
-def loop(count, step):
-    def run(i, carry):
-        step(i)
-        return carry
-
-    lax.fori_loop(0, count, run, 0)
 
 
 def each(count, step):
@@ -119,6 +114,7 @@
     xh2,
     r2,
     c_buf,
+    back_buf,
     g_buf,
     du_buf,
     dc_snd,
@@ -128,7 +124,9 @@
     da_snd,
     da_rcv,
     do_buf,
+    do_snd,
     dhb,
+    fo_buf,
     dp_buf,
     grads,
     r0_buf,
@@ -144,6 +142,8 @@
     o_recv,
     x_send,
     x_recv,
+    y_send,
+    y_recv,
     g_send,
     g_recv,
     v_send,
@@ -161,7 +161,6 @@
     pairs = local // (2 * HEAD)
     hidden = win.shape[1]
     scale = HEAD ** (-0.5)
-    blocks = count // BLOCK
     vacc = vsum.at[0]
 
     barrier = pltpu.get_barrier_semaphore()
@@ -240,14 +239,22 @@
         place = o_buf.at[t, here, cols(p, 128)]
         return across(place, place, o_send.at[s, p], o_recv.at[s, p])
 
+    half = length // 2
+
+    def mine(s):
+        return rows(2 * s + t, half)
+
+    def theirs(s):
+        return rows(2 * s + 1 - t, half)
+
     def dc_copy(n, i):
-        here = rows(n, BLOCK), cols(i, 256)
+        here = theirs(n), cols(i, 256)
         return across(
             dc_snd.at[here], dc_rcv.at[here], x_send.at[0, n, i], x_recv.at[0, n, i]
         )
 
     def da_copy(s, i):
-        here = rows(s, length), cols(i, 256)
+        here = theirs(s), cols(i, 256)
         return across(
             da_snd.at[here], da_rcv.at[here], x_send.at[1, s, i], x_recv.at[1, s, i]
         )
@@ -257,6 +264,16 @@
         return across(
             mlp_snd.at[here], mlp_rcv.at[here], x_send.at[2, s, i], x_recv.at[2, s, i]
         )
+
+    def do_copy(s):
+        return across(do_snd.at[rows(s, half)], do_buf.at[mine(s)], y_send.at[s], y_recv.at[s])
+
+    def gt_copy(s):
+        here = gtok_ref.at[mine(s)]
+        return across(here, here, y_send.at[2 + s], y_recv.at[2 + s])
+
+    def fo_copy():
+        return across(fo_buf.at[0], fo_buf.at[1], y_send.at[4], y_recv.at[4])
 
     wide = width // 256
 
@@ -310,7 +327,7 @@
 
         each(length // CHUNK, step)
 
-    def attention(s):
+    def attention(s, after):
         seq = rows(s, length)
         allowed = same_image(s)
 
@@ -337,6 +354,7 @@
                 both.astype(BF), stacked(mixed[:, 256:]), NN
             ).astype(BF)
             o_copy(s, p).start()
+            after(p)
 
         each(pairs, pair_step)
 
@@ -348,16 +366,19 @@
     wo_copy(0, 1).start()
     for copy in wq_loads:
         copy.wait()
-    attention(0)
-    wo_share(0)
-    wo_share(1)
-    attention(1)
+    attention(0, lambda p: None)
+
+    def bring(p):
+        if p > 0:
+            wo_share(p - 1)
+
+    attention(1, bring)
 
     strip = width // WAYS
     received = [r0_buf, r1_buf, r2_buf, r3_buf]
 
     def product(piece, left, right, order):
-        full = dot(left[...], right, TN)
+        full = dot(left, right, TN)
         for k in range(WAYS):
             b = [(k >> i) & 1 for i in order]
             grads[piece, b[0], b[1], b[2], b[3]] = full[k * strip : (k + 1) * strip].astype(BF)
@@ -387,28 +408,30 @@
 
     hidden_pieces = hidden // TILE
     down, into, outs, mixes = 0, hidden_pieces, 2 * hidden_pieces, 2 * hidden_pieces + 1
-    total = mixes + pairs
+    others = mixes + pairs
+    total = others + 1
 
     dy_load.wait()
-    vacc[4:5] += jnp.sum(dy[...].astype(F32), axis=0, keepdims=True)
+    vacc[3:4] += jnp.sum(dy[...].astype(F32), axis=0, keepdims=True)
+    wdn_load.wait()
+
+    def hidden_back(i):
+        back_buf[:, cols(i, 256)] = dot(dy[...], wdn[:, cols(i, 256)], NN)
+
+    each(hidden // 256, hidden_back)
     wo_load.wait()
     win_load.wait()
-    wdn_load.wait()
     for part in range(2):
         wo_forward(part)
     for part in range(2):
         wo_copy(1, part).wait_recv()
         wo_copy(3, part).wait_recv()
 
-    per = length // BLOCK
-
     def middle(n):
         here = rows(n, BLOCK)
 
-        @pl.when(lax.rem(n, per) == 0)
-        def _():
-            for p in range(pairs):
-                o_copy(n // per, p).wait_recv()
+        for p in range(pairs):
+            o_copy(n, p).wait_recv()
 
         h_buf[here] = dot(o_buf[0, here], wo[0], NT) + dot(o_buf[1, here], wo[1], NT)
 
@@ -429,27 +452,31 @@
                 there = cols(i, 256)
                 part = cols(m * wide + i, 256)
                 pre = dot(c_buf[here], win[:, part], NN) + vin[6 + m : 7 + m, there]
-                back = dot(dy[here], wdn[:, part], NN)
                 phi = 0.5 + 0.5 * lax.erf(pre * 0.7071067811865476)
                 g_buf[here, part] = (pre * phi).astype(BF)
                 slope = phi + pre * (jnp.exp(-0.5 * pre * pre) * 0.3989422804014327)
-                low = (back * slope).astype(BF)
+                low = (back_buf[here, part] * slope).astype(BF)
                 du_buf[here, part] = low
                 vacc[1 + m : 2 + m, there] += jnp.sum(low.astype(F32), axis=0, keepdims=True)
 
             each(wide, hidden_step)
+
+    def normed_back(n):
+        here = rows(n, BLOCK)
 
         def back_step(i):
             there = cols(i, 256)
             grad = dot(du_buf[here], win[rows(i, 256)], NT)
             dc_snd[here, there] = grad.astype(BF)
             dc_copy(n, i).start()
-            vacc[6:7, there] += jnp.sum(grad * xh2[here, there], axis=0, keepdims=True)
-            vacc[8:9, there] += jnp.sum(grad, axis=0, keepdims=True)
+            vacc[10:11, there] += jnp.sum(grad * xh2[here, there], axis=0, keepdims=True)
+            vacc[12:13, there] += jnp.sum(grad, axis=0, keepdims=True)
 
         each(wide, back_step)
 
-    loop(blocks, middle)
+    middle(0)
+    normed_back(0)
+    middle(1)
 
     def mlp_out(s):
         seq = rows(s, length)
@@ -461,24 +488,27 @@
         each(wide, step)
 
     def resid_back(s):
-        seq = rows(s, length)
-        for n in range(s * per, (s + 1) * per):
-            for i in range(wide):
-                dc_copy(n, i).wait_recv()
+        for i in range(wide):
+            dc_copy(s, i).wait_recv()
 
         def step(i):
-            here = rows(s * (length // CHUNK) + i, CHUNK)
+            here = rows((2 * s + t) * (half // CHUNK) + i, CHUNK)
             grad = dc_snd[here].astype(F32) + dc_rcv[here].astype(F32)
             full = dy[here].astype(F32) + norm_back(grad, xh2[here], r2[here], vin[1:2])
             xh2[here] = full
-            dhb[here] = full.astype(BF)
-            vacc[3:4] += jnp.sum(full, axis=0, keepdims=True)
-
-        each(length // CHUNK, step)
-        do_buf[seq] = dot(dhb[seq], wo[t], NN).astype(BF)
+            dhb[rows(s * (half // CHUNK) + i, CHUNK)] = full.astype(BF)
+            vacc[8:9] += jnp.sum(full, axis=0, keepdims=True)
+
+        each(half // CHUNK, step)
+        low = dhb[rows(s, half)]
+        do_snd[rows(s, half)] = dot(low, wo[1 - t], NN).astype(BF)
+        do_copy(s).start()
+        do_buf[mine(s)] = dot(low, wo[t], NN).astype(BF)
 
     def attention_back(s, p):
         seq = rows(s, length)
+        if (s, p) in heads_first:
+            do_copy(s).wait_recv()
         mixed = qkv[seq, cols(p, 384)]
         query, keys = mixed[:, :128], stacked(mixed[:, 128:256])
         grad_o = do_buf[seq, cols(p, 128)]
@@ -507,8 +537,8 @@
             here = cols(i, 256)
             grad = dot(dp_buf[seq], wq[rows(i, 256)], NT)
             da_snd[seq, here] = grad.astype(BF)
-            vacc[5:6, here] += jnp.sum(grad * xh1[seq, here], axis=0, keepdims=True)
-            vacc[7:8, here] += jnp.sum(grad, axis=0, keepdims=True)
+            vacc[9:10, here] += jnp.sum(grad * xh1[seq, here], axis=0, keepdims=True)
+            vacc[11:12, here] += jnp.sum(grad, axis=0, keepdims=True)
 
         each(wide, step)
 
@@ -532,25 +562,26 @@
             da_copy(s, i).wait_recv()
 
         def step(i):
-            here = rows(s * (length // CHUNK) + i, CHUNK)
+            here = rows((2 * s + t) * (half // CHUNK) + i, CHUNK)
             grad = da_snd[here].astype(F32) + da_rcv[here].astype(F32)
             full = xh2[here] + norm_back(grad, xh1[here], r1[here], vin[0:1])
             gtok_ref[here] = full.astype(BF)
 
-        each(length // CHUNK, step)
+        each(half // CHUNK, step)
+        gt_copy(s).start()
 
     def v_copy(k):
         sems = v_send.at[k], v_recv.at[k]
         if k == 0:
-            return across(vsum.at[0], vrcv.at[0], *sems)
+            shared = pl.ds(8, 8)
+            return across(vsum.at[0, shared], vrcv.at[0, shared], *sems)
         return toward(k - 1, vsum.at[k], vrcv.at[k], *sems)
 
     def v_next(k):
         v_copy(k).wait_recv()
         if k == 0:
-            line = lax.broadcasted_iota(jnp.int32, vacc.shape, 0)
-            norms = (line >= 5) & (line < 9)
-            vsum[1] = jnp.where(norms, vsum[0] + vrcv[0], vsum[0])
+            vsum[1, :8] = vsum[0, :8]
+            vsum[1, 8:] = vsum[0, 8:] + vrcv[0, 8:]
         else:
             vsum[k + 1] = vsum[k] + vrcv[k]
         if k < BITS:
@@ -559,13 +590,15 @@
     def prod(piece):
         order = HALVINGS[piece]
         if piece < into:
-            product(piece, dy, g_buf[:, cols(piece, TILE)], order)
+            product(piece, dy[...], g_buf[:, cols(piece, TILE)], order)
         elif piece < outs:
-            product(piece, c_buf, du_buf[:, cols(piece - into, TILE)], order)
-        elif piece < mixes:
-            product(piece, dhb, o_buf[t], order)
+            product(piece, c_buf[...], du_buf[:, cols(piece - into, TILE)], order)
+        elif piece in (outs, others):
+            side = t if piece == outs else 1 - t
+            heads = jnp.concatenate([o_buf[side, mine(s)] for s in range(seqs)], axis=0)
+            product(piece, dhb[...], heads, order)
         else:
-            product(piece, a_buf, dp_buf[:, cols(piece - mixes, 384)], order)
+            product(piece, a_buf[...], dp_buf[:, cols(piece - mixes, 384)], order)
 
     def fin(piece):
         value = finish(piece, HALVINGS[piece])
@@ -573,11 +606,24 @@
             gdn_ref[:, cols(piece, TILE)] = value
         elif piece < outs:
             gin_ref[:, cols(piece - into, TILE)] = value
-        elif piece < mixes:
-            gout_ref[...] = value
         else:
             for kind in range(3):
                 gqkv_ref[kind, :, cols(piece - mixes, 128)] = value[:, cols(kind, 128)]
+
+    def outer_send():
+        fo_buf[0] = finish(others, HALVINGS[others]).astype(BF)
+        fo_copy().start()
+
+    def outer_end():
+        value = finish(outs, HALVINGS[outs])
+        fo_copy().wait_recv()
+        gout_ref[...] = value + fo_buf[1].astype(F32)
+
+    heads_first = {}
+    for name, *which in PLAN:
+        if name == "attb":
+            heads_first.setdefault(which[0], tuple(which))
+    heads_first = tuple(heads_first.values())
 
     def small(k):
         if k == 0:
@@ -591,6 +637,7 @@
         "prod": prod,
         "pass": lambda piece, k: pass_on(piece, k, HALVINGS[piece]),
         "fin": fin,
+        "mb": normed_back,
         "resid": resid_back,
         "attb": attention_back,
         "mixb": mixed_back,
@@ -598,6 +645,9 @@
         "mlp": mlp_out,
         "fb": finish_block,
         "ft": finish_tokens,
+        "gt": lambda s: gt_copy(s).wait_recv(),
+        "fo": outer_send,
+        "foe": outer_end,
         "v": small,
     }
     for name, *which in PLAN:
@@ -612,10 +662,10 @@
         for i in range(wide):
             da_copy(s, i).wait_send()
             mlp_copy(s, i).wait_send()
-    for n in range(blocks):
-        for i in range(wide):
-            dc_copy(n, i).wait_send()
-
+            dc_copy(s, i).wait_send()
+        do_copy(s).wait_send()
+        gt_copy(s).wait_send()
+    fo_copy().wait_send()
     for piece in range(total):
         for k in range(BITS):
             g_copy(piece, k, HALVINGS[piece]).wait_send()
@@ -660,10 +710,10 @@
     pair_o[0:1] = small[0:1, :local]
     pair_o[1:2] = small[0:1, local:]
     hb_o[...] = jnp.concatenate([small[1:2], small[2:3]], axis=1).reshape(hidden)
-    ob_o[...] = small[3:4].reshape(width)
-    mb_o[...] = small[4:5].reshape(width)
-    gain_o[...] = small[5:7]
-    shift_o[...] = small[7:9]
+    ob_o[...] = small[8:9].reshape(width)
+    mb_o[...] = small[3:4].reshape(width)
+    gain_o[...] = small[9:11]
+    shift_o[...] = small[11:13]
     for copy in copies:
         copy.wait()
 
@@ -692,7 +742,7 @@
     pairs = local // (2 * HEAD)
     stride = dp // WAYS
     strip = width // WAYS
-    pieces = 2 * (hidden // TILE) + 1 + pairs
+    pieces = 2 * (hidden // TILE) + 2 + pairs
     hbm = pl.BlockSpec(memory_space=pl.ANY)
     vmem = pl.BlockSpec(memory_space=pltpu.VMEM)
     dma = pltpu.SemaphoreType.DMA
@@ -728,6 +778,7 @@
             pltpu.VMEM(wide, F32),
             pltpu.VMEM((count, 1), F32),
             pltpu.VMEM(wide, BF),
+            pltpu.VMEM((count, hidden), F32),
             pltpu.VMEM((count, hidden), BF),
             pltpu.VMEM((count, hidden), BF),
             pltpu.VMEM(wide, BF),
@@ -737,7 +788,9 @@
             pltpu.VMEM(wide, BF),
             pltpu.VMEM(wide, BF),
             pltpu.VMEM((count, local), BF),
-            pltpu.VMEM(wide, BF),
+            pltpu.VMEM((count // 2, local), BF),
+            pltpu.VMEM((count // 2, width), BF),
+            pltpu.VMEM((2, strip, local), BF),
             pltpu.VMEM((count, 3 * local), BF),
             pltpu.VMEM((pieces, 2, 2, 2, 2, strip, TILE), BF),
             pltpu.VMEM((pieces, 2, 2, 2, strip, TILE), BF),
@@ -753,13 +806,15 @@
             dma((seqs, pairs)),
             dma((3, count // BLOCK, width // 256)),
             dma((3, count // BLOCK, width // 256)),
+            dma((5,)),
+            dma((5,)),
             dma((pieces, BITS)),
             dma((pieces, BITS)),
             dma((BITS + 1,)),
             dma((BITS + 1,)),
         ],
         compiler_params=pltpu.CompilerParams(
-            collective_id=0, has_side_effects=True, vmem_limit_bytes=56 * 2**20
+            collective_id=0, has_side_effects=True, vmem_limit_bytes=58 * 2**20
         ),
         cost_estimate=pl.CostEstimate(
             flops=12 * 10**9, bytes_accessed=12 * 10**6, transcendentals=4 * 10**6

time: 76.5 us -> 75.5 us (0.987)
  Pallas kernels: 75.5 us -> 74.4 us
    pallas_call x1, Pallas kernels: 73.4 us -> 72.3 us  [body(): pl.pallas_call(functools.partial(kernel, stride), out_shape=big + (pltpu....]
where the time goes in v4:
time: 75.5 us; the launch traced here: 75.3 us
  Pallas kernels  74.4 us (99%)
  between operations  0.84 us (1%)
    pallas_call x1, Pallas kernels, body(): pl.pallas_call(functools.partial(kernel, stride), out_shape=big + (pltpu....  72.3 us
    pallas_call x1, Pallas kernels, body(): pl.pallas_call(deliver, out_shape=tuple((jax.ShapeDtypeStruct(v.shape, v....  2.1 us

profile of v4, /device:TPU:0, one launch (start us, length us, event | category | flops | bytes accessed | tf_op | source)
XLA Modules:
  0.0 75.3 jit_solution(8493832814759628891)
XLA Ops:
  0.6 72.3 %shard_map.220 = (bf16[512,768]{1,0:T(8,128)(2,1)S(1)}, bf16[512,768]{1,0:T(8,128)(2,1)S(1)}, f32[3,48,384]{2,1,0:T(8,128)S(1)}, f32[48,384]{1,0:T(8,128)S(1)}, ...) custom-call(bf16[512,768]{1,0:T(8,128)(2,1)} %bitcast.7, s32[2,256]{1,0:T(2,128)} %seg_ref.1, ...), custom_call_target="tpu_custom_call" | custom-call | flops 12000000000 | bytes 12000000 | tf_op jit(solution)/shard_map/pallas_call | solution.py:758
  73.0 2.1 %shard_map.221 = (bf16[512,768]{1,0:T(8,128)(2,1)}, bf16[512,768]{1,0:T(8,128)(2,1)}, f32[3,48,384]{2,1,0:T(8,128)}, f32[2,384]{1,0:T(2,128)}, f32[48,384]{1,0:T...) custom-call(bf16[512,768]{1,0:T(8,128)(2,1)S(1)} %get-tuple-element., ...), custom_call_target="tpu_custom_call" | custom-call | tf_op jit(solution)/shard_map/pallas_call | solution.py:863

commit v5 on v4

--- a/solution.py
+++ b/solution.py
@@ -693,6 +693,12 @@
     mb_o,
     gain_o,
     shift_o,
+    pair_m,
+    ob_m,
+    hb_m,
+    mb_m,
+    gain_m,
+    shift_m,
     sem,
 ):
     big = (
@@ -707,13 +713,24 @@
     for copy in copies:
         copy.start()
     local, width, hidden = pair_o.shape[1], ob_o.shape[0], hb_o.shape[0]
-    pair_o[0:1] = small[0:1, :local]
-    pair_o[1:2] = small[0:1, local:]
-    hb_o[...] = jnp.concatenate([small[1:2], small[2:3]], axis=1).reshape(hidden)
-    ob_o[...] = small[8:9].reshape(width)
-    mb_o[...] = small[3:4].reshape(width)
-    gain_o[...] = small[9:11]
-    shift_o[...] = small[11:13]
+    pair_m[0:1] = small[0:1, :local]
+    pair_m[1:2] = small[0:1, local:]
+    hb_m[...] = jnp.concatenate([small[1:2], small[2:3]], axis=1).reshape(hidden)
+    ob_m[...] = small[8:9].reshape(width)
+    mb_m[...] = small[3:4].reshape(width)
+    gain_m[...] = small[9:11]
+    shift_m[...] = small[11:13]
+    little = (
+        (pair_m, pair_o),
+        (ob_m, ob_o),
+        (hb_m, hb_o),
+        (mb_m, mb_o),
+        (gain_m, gain_o),
+        (shift_m, shift_o),
+    )
+    for i, (src, dst) in enumerate(little):
+        copies.append(pltpu.make_async_copy(src, dst, sem.at[len(big) + i]))
+        copies[-1].start()
     for copy in copies:
         copy.wait()
 
@@ -859,13 +876,12 @@
         jax.ShapeDtypeStruct((2, width), F32),
         jax.ShapeDtypeStruct((2, width), F32),
     ]
-    placed = [hbm, hbm, hbm, vmem, hbm, vmem, hbm, vmem, hbm, vmem, vmem, vmem]
     done = pl.pallas_call(
         deliver,
         out_shape=tuple(jax.ShapeDtypeStruct(v.shape, v.dtype) for v in shapes),
         in_specs=[vmem] * 7,
-        out_specs=tuple(placed),
-        scratch_shapes=[dma((6,))],
+        out_specs=(hbm,) * 12,
+        scratch_shapes=[pltpu.VMEM(shapes[i].shape, F32) for i in (3, 5, 7, 9, 10, 11)] + [dma((12,))],
     )(*[pltpu.with_memory_space_constraint(v, pltpu.VMEM) for v in outs])
     return (
         done[0].reshape(tokens.shape),

time: 75.5 us -> 74.9 us (level)
  no operation moved by 1% of the time
where the time goes in v5:
time: 74.9 us; the launch traced here: 74.7 us
  Pallas kernels  73.9 us (99%)
  between operations  0.84 us (1%)
    pallas_call x1, Pallas kernels, body(): pl.pallas_call(functools.partial(kernel, stride), out_shape=big + (pltpu....  72.3 us
    pallas_call x1, Pallas kernels, body(): pl.pallas_call(deliver, out_shape=tuple((jax.ShapeDtypeStruct(v.shape, v....  1.55 us

profile of v5, /device:TPU:0, one launch (start us, length us, event | category | flops | bytes accessed | tf_op | source)
XLA Modules:
  0.0 74.7 jit_solution(8331528640001708437)
XLA Ops:
  0.6 72.3 %shard_map.220 = (bf16[512,768]{1,0:T(8,128)(2,1)S(1)}, bf16[512,768]{1,0:T(8,128)(2,1)S(1)}, f32[3,48,384]{2,1,0:T(8,128)S(1)}, f32[48,384]{1,0:T(8,128)S(1)}, ...) custom-call(bf16[512,768]{1,0:T(8,128)(2,1)} %bitcast.7, s32[2,256]{1,0:T(2,128)} %seg_ref.1, ...), custom_call_target="tpu_custom_call" | custom-call | flops 12000000000 | bytes 12000000 | tf_op jit(solution)/shard_map/pallas_call | solution.py:775
  73.0 1.6 %shard_map.221 = (bf16[512,768]{1,0:T(8,128)(2,1)}, bf16[512,768]{1,0:T(8,128)(2,1)}, f32[3,48,384]{2,1,0:T(8,128)}, f32[2,384]{1,0:T(2,128)}, f32[48,384]{1,0:T...) custom-call(bf16[512,768]{1,0:T(8,128)(2,1)S(1)} %get-tuple-element., ...), custom_call_target="tpu_custom_call" | custom-call | tf_op jit(solution)/shard_map/pallas_call | solution.py:879

commit v6 on v5

--- a/solution.py
+++ b/solution.py
@@ -164,9 +164,9 @@
     vacc = vsum.at[0]
 
     barrier = pltpu.get_barrier_semaphore()
+    for b in reversed(range(BITS)):
+        pl.semaphore_signal(barrier, inc=1, device_id=(mate[b], t), device_id_type=MESH)
     pl.semaphore_signal(barrier, inc=1, device_id=(d, 1 - t), device_id_type=MESH)
-    for b in range(BITS):
-        pl.semaphore_signal(barrier, inc=1, device_id=(mate[b], t), device_id_type=MESH)
 
     loads = []
 

time: 74.9 us -> 74.9 us (level)
  no operation moved by 1% of the time
where the time goes in v6:
time: 74.9 us; the launch traced here: 74.7 us
  Pallas kernels  73.9 us (99%)
  between operations  0.84 us (1%)
    pallas_call x1, Pallas kernels, body(): pl.pallas_call(functools.partial(kernel, stride), out_shape=big + (pltpu....  72.3 us
    pallas_call x1, Pallas kernels, body(): pl.pallas_call(deliver, out_shape=tuple((jax.ShapeDtypeStruct(v.shape, v....  1.55 us

profile of v6, /device:TPU:0, one launch (start us, length us, event | category | flops | bytes accessed | tf_op | source)
XLA Modules:
  0.0 74.7 jit_solution(10002770299233638804)
XLA Ops:
  0.6 72.3 %shard_map.220 = (bf16[512,768]{1,0:T(8,128)(2,1)S(1)}, bf16[512,768]{1,0:T(8,128)(2,1)S(1)}, f32[3,48,384]{2,1,0:T(8,128)S(1)}, f32[48,384]{1,0:T(8,128)S(1)}, ...) custom-call(bf16[512,768]{1,0:T(8,128)(2,1)} %bitcast.7, s32[2,256]{1,0:T(2,128)} %seg_ref.1, ...), custom_call_target="tpu_custom_call" | custom-call | flops 12000000000 | bytes 12000000 | tf_op jit(solution)/shard_map/pallas_call | solution.py:775
  73.0 1.6 %shard_map.221 = (bf16[512,768]{1,0:T(8,128)(2,1)}, bf16[512,768]{1,0:T(8,128)(2,1)}, f32[3,48,384]{2,1,0:T(8,128)}, f32[2,384]{1,0:T(2,128)}, f32[48,384]{1,0:T...) custom-call(bf16[512,768]{1,0:T(8,128)(2,1)S(1)} %get-tuple-element., ...), custom_call_target="tpu_custom_call" | custom-call | tf_op jit(solution)/shard_map/pallas_call | solution.py:879
